TPU v7x, 128 devices: a whole 4x4x4 slice. The times are simulated.
128 devices in a mesh: lat: 8 (over y, z_lo), lon: 16 (over x, z_hi, core).
Axes of the slice: x: 4, y: 4, z: 4 (z_hi: 2, z_lo: 2; z = z_hi * 2 + z_lo), core: 2. Of those that a mesh axis runs over, the one named last changes fastest.
Arguments:
- atmos_features: bfloat16 [256, 512, 768], P('lat', 'lon'), may hold values from -6 to 6
- ocean_features: bfloat16 [512, 1024, 192], P('lat', 'lon'), may hold values from -6 to 6
- wet_cell_mask: int32 [512, 1024], P('lat', 'lon'), may hold values from 0 to 1, as said below
- overlay_cell_index: int32 [4, 512, 1024], P(None, 'lat', 'lon'), may hold values from 0 to 16383, as said below
- remap_weight: float32 [4, 512, 1024], P(None, 'lat', 'lon'), may hold values from 0.1 to 1
- query_key_value_weight: bfloat16 [768, 2304], replicated, may hold values from -5 to 5
- attention_out_weight: bfloat16 [768, 768], replicated, may hold values from -0.21875 to 0.21875
- feedforward_up_weight: bfloat16 [768, 3072], replicated, may hold values from -0.21875 to 0.21875
- feedforward_down_weight: bfloat16 [3072, 768], replicated, may hold values from -0.109375 to 0.109375
- attention_gain: float32 [768], replicated, may hold values from 0.25 to 1.75
- feedforward_gain: float32 [768], replicated, may hold values from 0.25 to 1.75
- flux_head_weight: bfloat16 [768, 8], replicated, may hold values from -0.21875 to 0.21875
- surface_temp_embedding: float32 [768], replicated, may hold values from -5 to 5
- forcing_lift_weight: float32 [8, 192], replicated, may hold values from -2 to 2
- depthwise_kernels: float32 [2, 49, 192], replicated, may hold values from -0.875 to 0.875
- ocean_norm_gains: float32 [2, 192], replicated, may hold values from 0.25 to 1.75
- ocean_up_weights: bfloat16 [2, 192, 768], replicated, may hold values from -0.4375 to 0.4375
- ocean_down_weights: bfloat16 [2, 768, 192], replicated, may hold values from -0.21875 to 0.21875
- surface_temp_head: float32 [192], replicated, may hold values from -0.4375 to 0.4375
Outputs:
- atmos_updated: bfloat16 [256, 512, 768], P('lat', 'lon')
- ocean_out: bfloat16 [512, 1024, 192], P('lat', 'lon')
Inputs may be any that keep to these rules, and one draw needn't show every extreme that they name: `wet_cell_mask`: the ocean tile of rows [i * 64, i * 64 + 64) and columns [j * 64, j * 64 + 64) and the tile 512 / 2 rows north or south of it in the same columns together hold at most 4096 wet cells; some pair holds exactly that many. `overlay_cell_index`: each entry names an atmosphere cell of the latitude band of the ocean row: ocean row r belongs to the band of atmosphere rows [(r // 64) * 32, (r // 64) * 32 + 32), and the entry is (row within the band) * 512 + column.
All inputs are finite; a program needn't handle non-finite values.
Results may differ from a plain program's by a relative error of at most 0.013.
Values may be sent and summed in bfloat16 or wider, within the bound.
A program may use at most 128 MiB of HBM per device.

v0:
```python
import jax
import jax.numpy as jnp
from jax import lax
from jax.sharding import PartitionSpec as P

HEADS = 12
HD = 64
WR = 8
WC = 16


EPS = 1e-06


def with_halo(block, sides, width):
    for axis, dim in sides:
        count = lax.axis_size(axis)
        forward = [(i, i + 1) for i in range(count - 1)]
        forward.append((count - 1, 0))
        backward = [(target, source) for source, target in forward]
        low = lax.ppermute(
            lax.slice_in_dim(block, block.shape[dim] - width, None, axis=dim), axis, forward
        )
        high = lax.ppermute(lax.slice_in_dim(block, 0, width, axis=dim), axis, backward)
        block = jnp.concatenate([low, block, high], axis=dim)
    return block


def from_everyone(array, axis):
    copies = jnp.broadcast_to(array, (lax.axis_size(axis), *array.shape))
    return lax.all_to_all(copies, axis, split_axis=0, concat_axis=0, tiled=True)


def laid_out(blocks, dim):
    blocks = jnp.moveaxis(blocks, 0, dim)
    shape = blocks.shape
    return blocks.reshape(*shape[:dim], shape[dim] * shape[dim + 1], *shape[dim + 2 :])


def collect(array, axis, dim):
    blocks = from_everyone(array, axis)
    return laid_out(blocks, dim)


def swapped(block, axis, apart):
    count = lax.axis_size(axis)
    route = []
    for low in range(count):
        high = low | 1 << apart
        if high != low and high < count:
            route += [(low, high), (high, low)]
    return lax.ppermute(block, axis, route)


def rms_scale(values, gain):
    return values * lax.rsqrt(jnp.mean(values * values, axis=-1, keepdims=True) + EPS) * gain


def layer_scale(values, gain):
    center = values - jnp.mean(values, axis=-1, keepdims=True)
    return center * lax.rsqrt(jnp.mean(center * center, axis=-1, keepdims=True) + EPS) * gain


def to_windows(tensor):
    row_total, column_total = (tensor.shape[0], tensor.shape[1])
    shaped = tensor.reshape(row_total // WR, WR, column_total // WC, WC, HEADS, HD)
    return shaped.transpose(0, 2, 4, 1, 3, 5).reshape(-1, HEADS, WR * WC, HD)


def from_windows(tensor, row_total, column_total):
    shaped = tensor.reshape(row_total // WR, column_total // WC, HEADS, WR, WC, HD)
    return shaped.transpose(0, 3, 1, 4, 2, 5).reshape(row_total, column_total, HEADS * HD)


def depthwise(padded, taps, row_total, column_total):
    total = jnp.zeros((row_total, column_total, padded.shape[2]), jnp.float32)
    for north in range(7):
        for east in range(7):
            window = padded[north : north + row_total, east : east + column_total].astype(
                jnp.float32
            )
            total = total + window * taps[north * 7 + east]
    return total


def ocean_mlp(normed, up_weight, down_weight):
    active = jax.nn.gelu(jnp.dot(normed, up_weight, preferred_element_type=jnp.float32)).astype(
        jnp.bfloat16
    )
    return jnp.dot(active, down_weight, preferred_element_type=jnp.float32)


def body(
    atmos_features,
    ocean_features,
    wet_cell_mask,
    overlay_cell_index,
    remap_weight,
    query_key_value_weight,
    attention_out_weight,
    feedforward_up_weight,
    feedforward_down_weight,
    attention_gain,
    feedforward_gain,
    flux_head_weight,
    surface_temp_embedding,
    forcing_lift_weight,
    depthwise_kernels,
    ocean_norm_gains,
    ocean_up_weights,
    ocean_down_weights,
    surface_temp_head,
):
    row_total, column_total, width = atmos_features.shape
    half_window = WC // 2
    model_state = atmos_features.astype(jnp.float32)
    normed = rms_scale(model_state, attention_gain).astype(jnp.bfloat16)
    query = jnp.dot(
        normed, query_key_value_weight[:, :width], preferred_element_type=jnp.float32
    ).astype(jnp.bfloat16)
    own_pairs = jnp.dot(
        normed, query_key_value_weight[:, width:], preferred_element_type=jnp.float32
    ).astype(jnp.bfloat16)
    key_value = with_halo(own_pairs, (("lon", 1),), half_window)
    query_wide = jnp.pad(query, ((0, 0), (half_window, half_window), (0, 0)))
    query_win = to_windows(query_wide)
    keys_win = to_windows(key_value[..., :width])
    value_win = to_windows(key_value[..., width:])
    scores = jnp.einsum(
        "whqd,whkd->whqk", query_win, keys_win, preferred_element_type=jnp.float32
    ) * HD ** (-0.5)
    probs = jax.nn.softmax(scores, axis=-1).astype(jnp.bfloat16)
    mixed = jnp.einsum(
        "whqk,whkd->whqd", probs, value_win, preferred_element_type=jnp.float32
    ).astype(jnp.bfloat16)
    attended = from_windows(mixed, row_total, column_total + WC)[
        :, half_window : half_window + column_total
    ]
    first = model_state + jnp.dot(
        attended, attention_out_weight, preferred_element_type=jnp.float32
    )
    normed_mlp = rms_scale(first, feedforward_gain).astype(jnp.bfloat16)
    active = jax.nn.gelu(
        jnp.dot(normed_mlp, feedforward_up_weight, preferred_element_type=jnp.float32)
    ).astype(jnp.bfloat16)
    second_half = first + jnp.dot(
        active, feedforward_down_weight, preferred_element_type=jnp.float32
    )
    fluxes = jnp.dot(
        second_half.astype(jnp.bfloat16), flux_head_weight, preferred_element_type=jnp.float32
    ).astype(jnp.bfloat16)
    band_flux = collect(fluxes, "lon", 1)
    band_flat = band_flux.reshape(-1, band_flux.shape[2])
    picked = band_flat[overlay_cell_index].astype(jnp.float32)
    forcing = jnp.sum(remap_weight[..., None] * picked, axis=0)
    ocean_rows, ocean_cols, channels = ocean_features.shape
    wet = wet_cell_mask.astype(jnp.float32)[..., None]
    lifted = jnp.dot(forcing, forcing_lift_weight, preferred_element_type=jnp.float32)
    ocean_field = wet * (ocean_features.astype(jnp.float32) + lifted)
    lat_index = lax.axis_index("lat")
    lat_count = lax.axis_size("lat")
    lon_count = lax.axis_size("lon")
    for block_id in range(depthwise_kernels.shape[0]):
        rounded = ocean_field.astype(jnp.bfloat16)
        padded = with_halo(rounded, (("lat", 0), ("lon", 1)), 3)
        top_rows = padded[ocean_rows : ocean_rows + 3]
        folded = top_rows[::-1, ::-1]
        for bit_index in range(lon_count.bit_length() - 1):
            folded = swapped(folded, "lon", bit_index)
        north_rows = jnp.where(lat_index == lat_count - 1, folded, padded[ocean_rows + 3 :])
        south_rows = jnp.where(lat_index == 0, jnp.zeros_like(padded[:3]), padded[:3])
        padded = jnp.concatenate([south_rows, padded[3 : ocean_rows + 3], north_rows], axis=0)
        convolved = depthwise(padded, depthwise_kernels[block_id], ocean_rows, ocean_cols)
        normed_ocean = layer_scale(convolved, ocean_norm_gains[block_id]).astype(jnp.bfloat16)
        increment = ocean_mlp(
            normed_ocean, ocean_up_weights[block_id], ocean_down_weights[block_id]
        )
        ocean_field = ocean_field + wet * increment
    ocean_out = ocean_field.astype(jnp.bfloat16)
    sea_surface_temp = jnp.dot(ocean_field, surface_temp_head, preferred_element_type=jnp.float32)
    numerator = sea_surface_temp.reshape(row_total, 2, column_total, 2).sum(axis=(1, 3))
    wet_cell_count = (
        wet_cell_mask.reshape(row_total, 2, column_total, 2).sum(axis=(1, 3)).astype(jnp.float32)
    )
    surface_temp_atmos = numerator / jnp.maximum(wet_cell_count, 1.0)
    atmos_updated = (second_half + surface_temp_atmos[..., None] * surface_temp_embedding).astype(
        jnp.bfloat16
    )
    return (atmos_updated, ocean_out)


def solution(mesh):
    in_specs = (
        P("lat", "lon", None),
        P("lat", "lon", None),
        P("lat", "lon"),
        P(None, "lat", "lon"),
        P(None, "lat", "lon"),
        P(),
        P(),
        P(),
        P(),
        P(),
        P(),
        P(),
        P(),
        P(),
        P(),
        P(),
        P(),
        P(),
        P(),
    )
    out_specs = (P("lat", "lon", None), P("lat", "lon", None))
    return jax.shard_map(body, mesh=mesh, in_specs=in_specs, out_specs=out_specs, check_vma=False)
```

profile of v0, /device:TPU:56, one launch (start us, length us, event | category | flops | bytes accessed | tf_op | source)
XLA Modules:
  0.0 461.8 jit_solution(12403716102495648522)
XLA Ops:
  2.6 4.9 %convolution_convert_fusion = bf16[32,32,1536]{2,1,0:T(8,128)(2,1)S(1)} fusion(bf16[768,2304]{1,0:T(8,128)(2,1)} %param.24, bf16[32,32,768]{2,1,0:T(8,128)(2,1)} %param.19, f32[768]{0:T(1024)} %param.28, f32[32,32]{1,0:T(8,128)S(1)} %add_rsqrt_fusion.3), kind=kOutput, calls=%fused_computation.138 | convolution fusion | flops 2420637696 | bytes 7086080 | tf_op jit(solution)/shard_map/dot_general | solution.py:121
  8.9 5.8 %collective-permute-start.1 = (bf16[32,8,1536]{2,1,0:T(8,128)(2,1)}, bf16[32,8,1536]{2,1,0:T(8,128)(2,1)}, u32[]{:S(2)}, u32[]{:S(2)}) collective-permute-start(bf16[32,8,1536]{2,1,0:T(8,128)(2,1)} %get-tuple-element.9), channel_id=1, source_target_pairs={{1,0},{2,1},{3,2},{4,3},{5,4},{6,5},{7,6},{8,7},{9,8},{10,9},{11,1... | collective-permute-start | bytes 2359304 | tf_op jit(solution)/shard_map/ppermute | solution.py:24
  17.6 6.0 %reshape.286 = bf16[4,8,3,16,12,64]{5,4,3,2,1,0:T(8,128)(2,1)} reshape(bf16[32,48,768]{2,1,0:T(8,128)(2,1)S(1)} %pad.4) | data formatting | bytes 4718592 | tf_op jit(solution)/shard_map/reshape | solution.py:66
  23.6 6.4 %copy.37 = bf16[4,3,12,8,16,64]{5,4,3,2,1,0:T(8,128)(2,1)} copy(bf16[4,3,12,8,16,64]{5,2,4,1,3,0:T(8,128)(2,1)} %bitcast.186) | data formatting | bytes 4718592 | tf_op jit(solution)/shard_map/transpose | solution.py:67
  35.1 8.2 %reshape.288 = bf16[4,8,3,16,12,64]{5,4,3,2,1,0:T(8,128)(2,1)} reshape(bf16[32,48,768]{2,1,0:T(8,128)(2,1)} %get-tuple-element.6) | data formatting | bytes 4718592 | tf_op jit(solution)/shard_map/reshape | solution.py:66
  43.3 6.3 %copy.38 = bf16[4,3,12,8,16,64]{5,4,3,2,1,0:T(8,128)(2,1)} copy(bf16[4,3,12,8,16,64]{5,2,4,1,3,0:T(8,128)(2,1)} %bitcast.187) | data formatting | bytes 4718592 | tf_op jit(solution)/shard_map/transpose | solution.py:67
  49.6 5.9 %reshape.290 = bf16[4,8,3,16,12,64]{5,4,3,2,1,0:T(8,128)(2,1)} reshape(bf16[32,48,768]{2,1,0:T(8,128)(2,1)S(1)} %get-tuple-element.7) | data formatting | bytes 4718592 | tf_op jit(solution)/shard_map/reshape | solution.py:66
  55.5 6.2 %copy.41 = bf16[4,3,12,8,16,64]{5,4,3,2,1,0:T(8,128)(2,1)} copy(bf16[4,3,12,8,16,64]{5,2,4,1,3,0:T(8,128)(2,1)} %bitcast.188) | data formatting | bytes 4718592 | tf_op jit(solution)/shard_map/transpose | solution.py:67
  61.8 11.8 %fusion.207 = (f32[12,12,128]{2,1,0:T(8,128)}, f32[12,12,128,128]{2,3,1,0:T(8,128)}) fusion(bf16[12,12,128,64]{3,2,1,0:T(8,128)(2,1)} %bitcast.191, bf16[12,12,128,64]{3,2,1,0:T(8,128)(2,1)} %bitcast.192), kind=kOutput, calls=%fused_computation.362 | convolution fusion | flops 309067904 | bytes 14229504 | tf_op jit(solution)/shard_map/sub | solution.py:132
  73.6 6.6 %fusion.142 = bf16[12,12,128,64]{2,3,1,0:T(8,128)(2,1)S(1)} fusion(bf16[12,12,128,64]{3,2,1,0:T(8,128)(2,1)} %bitcast.193, f32[12,12,128,128]{2,3,1,0:T(8,128)} %get-tuple-element.127, f32[12,12,128]{2,1,0:T(8,128)} %get-tuple-element.126), kind=kOutput, calls=%fused_computation.292 | convolution fusion | flops 307888128 | bytes 14229504 | tf_op jit(solution)/shard_map/whqk,whkd->whqd/dot_general | solution.py:133
  84.4 10.7 %copy.45 = bf16[4,8,3,16,12,64]{5,4,3,2,1,0:T(8,128)(2,1)} copy(bf16[4,8,3,16,12,64]{5,3,1,4,2,0:T(8,128)(2,1)} %bitcast.189) | data formatting | bytes 4718592 | tf_op jit(solution)/shard_map/transpose | solution.py:72
  95.0 7.2 %reshape.293 = bf16[32,48,768]{2,1,0:T(8,128)(2,1)S(1)} reshape(bf16[4,8,3,16,12,64]{5,4,3,2,1,0:T(8,128)(2,1)} %copy.45) | data formatting | bytes 4718592 | tf_op jit(solution)/shard_map/reshape | solution.py:72
  105.4 7.5 %fusion.36 = f32[32,32,3072]{2,1,0:T(8,128)S(1)} fusion(bf16[768,3072]{1,0:T(8,128)(2,1)} %param.26, f32[32,32,768]{2,1,0:T(8,128)S(1)} %get-tuple-element.129, f32[768]{0:T(1024)S(1)} %copy-done.69, f32[32,32]{1,0:T(8,128)S(1)} %add_rsqrt_fusion.2), kind=kOutput, calls=%fused_computation.123 | convolution fusion | flops 4834197504 | bytes 20454400 | tf_op jit(solution)/shard_map/dot_general | solution.py:144
  113.0 7.4 %fusion.145 = f32[32,32,768]{2,1,0:T(8,128)S(1)} fusion(f32[32,32,768]{2,1,0:T(8,128)S(1)} %get-tuple-element.129, bf16[3072,768]{1,0:T(8,128)(2,1)S(1)} %bitcast.297, f32[32,32,3072]{2,1,0:T(8,128)S(1)} %fusion.36), kind=kOutput, calls=%fused_computation.293 | convolution fusion | flops 4860936192 | bytes 23592960 | tf_op jit(solution)/shard_map/dot_general | solution.py:146
  125.0 6.7 %all-to-all-start = ((bf16[16,2,4096]{2,1,0:T(2,128)(2,1)}), bf16[16,2,4096]{2,1,0:T(2,128)(2,1)S(1)}, u32[]{:S(2)}, u32[]{:S(2)}) async-start(bf16[16,2,4096]{2,1,0:T(2,128)(2,1)} %reshape.320), calls=%async_computation | async-start | bytes 524288 | tf_op jit(solution)/shard_map/all_to_all | solution.py:31
  132.4 8.5 %all-to-all-done = bf16[16,2,4096]{2,1,0:T(2,128)(2,1)S(1)} async-done(((bf16[16,2,4096]{2,1,0:T(2,128)(2,1)}), bf16[16,2,4096]{2,1,0:T(2,128)(2,1)S(1)}, u32[]{:S(2)}, u32[]{:S(2)}) %all-to-all-start) | async-done | bytes 262176 | tf_op jit(solution)/shard_map/all_to_all | solution.py:31
  144.7 58.1 %gather_fusion = bf16[16384,8]{1,0:T(8,128)(2,1)} fusion(bf16[16384,8]{1,0:T(8,128)(2,1)} %bitcast.185, s32[16384]{0:T(1024)S(1)} %broadcast_clamp_fusion), kind=kCustom, calls=%fused_computation | custom fusion | bytes 589824 | tf_op jit(solution)/shard_map/gather | solution.py:154
  202.8 4.8 %fusion.25 = bf16[64,64,8]{2,1,0:T(8,128)(2,1)S(1)} fusion(bf16[4,64,64,8]{3,2,1,0:T(8,128)(2,1)} %bitcast.190, f32[4,64,64]{2,1,0:T(8,128)S(1)} %copy-done.14), kind=kLoop, calls=%fused_computation.112 | loop fusion | flops 360448 | bytes 393216 | tf_op jit(solution)/shard_map/reduce_sum | solution.py:155
  217.9 5.3 %collective-permute-start.5 = (bf16[70,3,192]{2,1,0:T(4,128)(2,1)S(1)}, bf16[70,3,192]{2,1,0:T(4,128)(2,1)S(1)}, u32[]{:S(2)}, u32[]{:S(2)}) collective-permute-start(bf16[70,3,192]{2,1,0:T(4,128)(2,1)S(1)} %get-tuple-element.21), channel_id=1, source_target_pairs={{1,0},{2,1},{3,2},{4,3},{5,4},{6,5},{7,6},{8,7},{9,8},{10,9},{11,1... | collective-permute-start | bytes 241928 | tf_op jit(solution)/shard_map/ppermute | solution.py:24
  245.8 74.1 %fusion.195 = (f32[64,64]{1,0:T(8,128)S(1)}, f32[64,64,192]{2,1,0:T(8,128)S(1)}) fusion(f32[192]{0:T(256)S(1)} %bitcast.242, bf16[3,70,192]{2,1,0:T(8,128)(2,1)S(1)} %get-tuple-element.13, bf16[64,70,192]{2,1,0:T(8,128)(2,1)} %slice.1213, f32[192]{0:T(256)S(1)} %bitcast.243, f32[192]{0:T(256)S(1)} %bitcast.244, f32[192]{0:T(256)S(1)} %bitcast.245, ...), kind=kLoop, calls=%fused_computation.350 | loop fusion | flops 214691840 | bytes 16091392 | tf_op jit(solution)/shard_map/reduce_sum | solution.py:60
  322.0 9.9 %fusion.208 = (bf16[64,64,192]{2,1,0:T(8,128)(2,1)S(1)}, f32[64,64,192]{2,1,0:T(8,128)}) fusion(bf16[2,768,192]{1,2,0:T(8,128)(2,1)S(1)} %copy-done.66, f32[64,64,192]{2,1,0:T(8,128)} %copy-done.2, f32[192]{0:T(256)S(1)} %bitcast.295, f32[64,64]{1,0:T(8,128)S(1)} %add_rsqrt_fusion.1, f32[64,64]{1,0:T(8,128)S(1)} %broadcast_multiply_fusion.1, ...), kind=kOutput, calls=%fused_computation.363 | convolution fusion | flops 2452094976 | bytes 15893504 | tf_op jit(solution)/shard_map/dot_general | solution.py:90
  340.7 5.3 %collective-permute-start.13 = (bf16[70,3,192]{2,1,0:T(4,128)(2,1)S(1)}, bf16[70,3,192]{2,1,0:T(4,128)(2,1)S(1)}, u32[]{:S(2)}, u32[]{:S(2)}) collective-permute-start(bf16[70,3,192]{2,1,0:T(4,128)(2,1)S(1)} %get-tuple-element.17), channel_id=1, source_target_pairs={{1,0},{2,1},{3,2},{4,3},{5,4},{6,5},{7,6},{8,7},{9,8},{10,9},{11,1... | collective-permute-start | bytes 241928 | tf_op jit(solution)/shard_map/ppermute | solution.py:24
  370.2 74.1 %fusion.194 = (f32[64,64]{1,0:T(8,128)S(1)}, f32[64,64,192]{2,1,0:T(8,128)S(1)}) fusion(f32[192]{0:T(256)S(1)} %bitcast.195, bf16[3,70,192]{2,1,0:T(8,128)(2,1)S(1)} %get-tuple-element.11, bf16[64,70,192]{2,1,0:T(8,128)(2,1)} %slice.1302, f32[192]{0:T(256)S(1)} %bitcast.196, f32[192]{0:T(256)S(1)} %bitcast.272, f32[192]{0:T(256)S(1)} %bitcast.273, ...), kind=kLoop, calls=%fused_computation.349 | loop fusion | flops 214691840 | bytes 16091392 | tf_op jit(solution)/shard_map/reduce_sum | solution.py:60
  447.7 7.8 %multiply_add_fusion = bf16[64,64,192]{2,1,0:T(8,128)(2,1)S(1)} fusion(f32[64,64,192]{2,1,0:T(8,128)} %get-tuple-element.133, f32[64,64]{1,0:T(8,128)S(1)} %convert_element_type.374, f32[64,64,192]{2,1,0:T(8,128)} %copy-done.3, f32[192]{0:T(256)S(1)} %bitcast.294, f32[64,64]{1,0:T(8,128)S(1)} %add_rsqrt_fusion, f32[64,64]{1,0:T(8,128)S(1)} %broadcast_multiply_fusion, ...), kind=kOutput, calls=%fused_computation.129 | convolution fusion | flops 2449735680 | bytes 10650624 | tf_op jit(solution)/shard_map/dot_general | solution.py:90
  (235 shorter events, 103.9 us)
Async XLA Ops:
  0.6 101.6 %copy-start = (bf16[768,768]{1,0:T(8,128)(2,1)S(1)}, bf16[768,768]{1,0:T(8,128)(2,1)}, u32[]{:S(2)}) copy-start(bf16[768,768]{1,0:T(8,128)(2,1)} %param.25) | copy-start | bytes 3538948
  2.5 12.2 %copy-start.10 = (bf16[32,32,768]{2,1,0:T(8,128)(2,1)S(1)}, bf16[32,32,768]{2,1,0:T(8,128)(2,1)}, u32[]{:S(2)}) copy-start(bf16[32,32,768]{2,1,0:T(8,128)(2,1)} %param.19) | copy-start | bytes 4718596
  2.6 12.2 %copy-start.68 = (f32[768]{0:T(1024)S(1)}, f32[768]{0:T(1024)}, u32[]{:S(2)}) copy-start(f32[768]{0:T(1024)} %param.28) | copy-start | bytes 9220
  8.9 21.8 %collective-permute-start = (bf16[32,8,1536]{2,1,0:T(8,128)(2,1)}, bf16[32,8,1536]{2,1,0:T(8,128)(2,1)}, u32[]{:S(2)}, u32[]{:S(2)}) collective-permute-start(bf16[32,8,1536]{2,1,0:T(8,128)(2,1)} %get-tuple-element.8), channel_id=1, source_target_pairs={{0,1},{1,2},{2,3},{3,4},{4,5},{5,6},{6,7},{7,8},{8,9},{9,10},{10,1... | collective-permute-start | bytes 2359304 | tf_op jit(solution)/shard_map/ppermute | solution.py:21
  8.9 21.8 %collective-permute-start.1 = (bf16[32,8,1536]{2,1,0:T(8,128)(2,1)}, bf16[32,8,1536]{2,1,0:T(8,128)(2,1)}, u32[]{:S(2)}, u32[]{:S(2)}) collective-permute-start(bf16[32,8,1536]{2,1,0:T(8,128)(2,1)} %get-tuple-element.9), channel_id=1, source_target_pairs={{1,0},{2,1},{3,2},{4,3},{5,4},{6,5},{7,6},{8,7},{9,8},{10,9},{11,1... | collective-permute-start | bytes 2359304 | tf_op jit(solution)/shard_map/ppermute | solution.py:24
  125.0 15.9 %all-to-all-start = ((bf16[16,2,4096]{2,1,0:T(2,128)(2,1)}), bf16[16,2,4096]{2,1,0:T(2,128)(2,1)S(1)}, u32[]{:S(2)}, u32[]{:S(2)}) async-start(bf16[16,2,4096]{2,1,0:T(2,128)(2,1)} %reshape.320), calls=%async_computation | async-start | bytes 524288 | tf_op jit(solution)/shard_map/all_to_all | solution.py:31
  144.7 58.1 %copy-start.14 = (f32[4,64,64]{2,1,0:T(8,128)S(1)}, f32[4,64,64]{2,1,0:T(8,128)}, u32[]{:S(2)}) copy-start(f32[4,64,64]{2,1,0:T(8,128)} %param.23) | copy-start | bytes 196612
  210.2 19.3 %copy-start.63 = (f32[2,192]{1,0:T(2,128)S(1)}, f32[2,192]{1,0:T(2,128)}, u32[]{:S(2)}) copy-start(f32[2,192]{1,0:T(2,128)} %param.34) | copy-start | bytes 4612
  210.3 4.9 %collective-permute-start.2 = (bf16[3,64,192]{2,1,0:T(8,128)(2,1)S(1)}, bf16[3,64,192]{2,1,0:T(8,128)(2,1)S(1)}, u32[]{:S(2)}, u32[]{:S(2)}) collective-permute-start(bf16[3,64,192]{2,1,0:T(8,128)(2,1)S(1)} %get-tuple-element.24), channel_id=1, source_target_pairs={{0,16},{16,32},{32,48},{48,64},{64,80},{80,96},{96,112},{112,0},{1... | collective-permute-start | bytes 221192 | tf_op jit(solution)/shard_map/ppermute | solution.py:21
  211.0 6.7 %collective-permute-start.3 = (bf16[3,64,192]{2,1,0:T(8,128)(2,1)S(1)}, bf16[3,64,192]{2,1,0:T(8,128)(2,1)S(1)}, u32[]{:S(2)}, u32[]{:S(2)}) collective-permute-start(bf16[3,64,192]{2,1,0:T(8,128)(2,1)S(1)} %get-tuple-element.25), channel_id=1, source_target_pairs={{16,0},{32,16},{48,32},{64,48},{80,64},{96,80},{112,96},{0,112},{1... | collective-permute-start | bytes 221192 | tf_op jit(solution)/shard_map/ppermute | solution.py:24
  217.8 8.3 %collective-permute-start.4 = (bf16[70,3,192]{2,1,0:T(4,128)(2,1)S(1)}, bf16[70,3,192]{2,1,0:T(4,128)(2,1)S(1)}, u32[]{:S(2)}, u32[]{:S(2)}) collective-permute-start(bf16[70,3,192]{2,1,0:T(4,128)(2,1)S(1)} %get-tuple-element.20), channel_id=1, source_target_pairs={{0,1},{1,2},{2,3},{3,4},{4,5},{5,6},{6,7},{7,8},{8,9},{9,10},{10,1... | collective-permute-start | bytes 241928 | tf_op jit(solution)/shard_map/ppermute | solution.py:21
  217.9 8.2 %collective-permute-start.5 = (bf16[70,3,192]{2,1,0:T(4,128)(2,1)S(1)}, bf16[70,3,192]{2,1,0:T(4,128)(2,1)S(1)}, u32[]{:S(2)}, u32[]{:S(2)}) collective-permute-start(bf16[70,3,192]{2,1,0:T(4,128)(2,1)S(1)} %get-tuple-element.21), channel_id=1, source_target_pairs={{1,0},{2,1},{3,2},{4,3},{5,4},{6,5},{7,6},{8,7},{9,8},{10,9},{11,1... | collective-permute-start | bytes 241928 | tf_op jit(solution)/shard_map/ppermute | solution.py:24
  226.5 1.4 collective-permute-start.6
  227.9 6.6 %collective-permute-start.7 = (bf16[3,70,192]{2,1,0:T(8,128)(2,1)S(1)}, bf16[3,70,192]{2,1,0:T(8,128)(2,1)S(1)}, u32[]{:S(2)}, u32[]{:S(2)}) collective-permute-start(bf16[3,70,192]{2,1,0:T(8,128)(2,1)S(1)} %collective-permute-done.6), channel_id=1, source_target_pairs={{0,2},{2,0},{1,3},{3,1},{4,6},{6,4},{5,7},{7,5},{8,10},{10,8},{9,1... | collective-permute-start | bytes 241928 | tf_op jit(solution)/shard_map/ppermute | solution.py:52
  234.5 4.7 %collective-permute-start.8 = (bf16[3,70,192]{2,1,0:T(8,128)(2,1)S(1)}, bf16[3,70,192]{2,1,0:T(8,128)(2,1)S(1)}, u32[]{:S(2)}, u32[]{:S(2)}) collective-permute-start(bf16[3,70,192]{2,1,0:T(8,128)(2,1)S(1)} %collective-permute-done.7), channel_id=1, source_target_pairs={{0,4},{4,0},{1,5},{5,1},{2,6},{6,2},{3,7},{7,3},{8,12},{12,8},{9,1... | collective-permute-start | bytes 241928 | tf_op jit(solution)/shard_map/ppermute | solution.py:52
  239.3 6.4 %collective-permute-start.9 = (bf16[3,70,192]{2,1,0:T(8,128)(2,1)S(1)}, bf16[3,70,192]{2,1,0:T(8,128)(2,1)S(1)}, u32[]{:S(2)}, u32[]{:S(2)}) collective-permute-start(bf16[3,70,192]{2,1,0:T(8,128)(2,1)S(1)} %collective-permute-done.8), channel_id=1, source_target_pairs={{0,8},{8,0},{1,9},{9,1},{2,10},{10,2},{3,11},{11,3},{4,12},{12,4},... | collective-permute-start | bytes 241928 | tf_op jit(solution)/shard_map/ppermute | solution.py:52
  331.9 5.7 %collective-permute-start.10 = (bf16[3,64,192]{2,1,0:T(8,128)(2,1)S(1)}, bf16[3,64,192]{2,1,0:T(8,128)(2,1)S(1)}, u32[]{:S(2)}, u32[]{:S(2)}) collective-permute-start(bf16[3,64,192]{2,1,0:T(8,128)(2,1)S(1)} %get-tuple-element.22), channel_id=1, source_target_pairs={{0,16},{16,32},{32,48},{48,64},{64,80},{80,96},{96,112},{112,0},{1... | collective-permute-start | bytes 221192 | tf_op jit(solution)/shard_map/ppermute | solution.py:21
  333.7 6.7 %collective-permute-start.11 = (bf16[3,64,192]{2,1,0:T(8,128)(2,1)S(1)}, bf16[3,64,192]{2,1,0:T(8,128)(2,1)S(1)}, u32[]{:S(2)}, u32[]{:S(2)}) collective-permute-start(bf16[3,64,192]{2,1,0:T(8,128)(2,1)S(1)} %get-tuple-element.23), channel_id=1, source_target_pairs={{16,0},{32,16},{48,32},{64,48},{80,64},{96,80},{112,96},{0,112},{1... | collective-permute-start | bytes 221192 | tf_op jit(solution)/shard_map/ppermute | solution.py:24
  340.6 8.3 %collective-permute-start.12 = (bf16[70,3,192]{2,1,0:T(4,128)(2,1)S(1)}, bf16[70,3,192]{2,1,0:T(4,128)(2,1)S(1)}, u32[]{:S(2)}, u32[]{:S(2)}) collective-permute-start(bf16[70,3,192]{2,1,0:T(4,128)(2,1)S(1)} %get-tuple-element.16), channel_id=1, source_target_pairs={{0,1},{1,2},{2,3},{3,4},{4,5},{5,6},{6,7},{7,8},{8,9},{9,10},{10,1... | collective-permute-start | bytes 241928 | tf_op jit(solution)/shard_map/ppermute | solution.py:21
  340.7 8.2 %collective-permute-start.13 = (bf16[70,3,192]{2,1,0:T(4,128)(2,1)S(1)}, bf16[70,3,192]{2,1,0:T(4,128)(2,1)S(1)}, u32[]{:S(2)}, u32[]{:S(2)}) collective-permute-start(bf16[70,3,192]{2,1,0:T(4,128)(2,1)S(1)} %get-tuple-element.17), channel_id=1, source_target_pairs={{1,0},{2,1},{3,2},{4,3},{5,4},{6,5},{7,6},{8,7},{9,8},{10,9},{11,1... | collective-permute-start | bytes 241928 | tf_op jit(solution)/shard_map/ppermute | solution.py:24
  349.3 2.2 collective-permute-start.14
  351.4 7.1 %collective-permute-start.15 = (bf16[3,70,192]{2,1,0:T(8,128)(2,1)}, bf16[3,70,192]{2,1,0:T(8,128)(2,1)}, u32[]{:S(2)}, u32[]{:S(2)}) collective-permute-start(bf16[3,70,192]{2,1,0:T(8,128)(2,1)} %collective-permute-done.14), channel_id=1, source_target_pairs={{0,2},{2,0},{1,3},{3,1},{4,6},{6,4},{5,7},{7,5},{8,10},{10,8},{9,1... | collective-permute-start | bytes 241928 | tf_op jit(solution)/shard_map/ppermute | solution.py:52
  358.5 5.0 %collective-permute-start.16 = (bf16[3,70,192]{2,1,0:T(8,128)(2,1)}, bf16[3,70,192]{2,1,0:T(8,128)(2,1)S(1)}, u32[]{:S(2)}, u32[]{:S(2)}) collective-permute-start(bf16[3,70,192]{2,1,0:T(8,128)(2,1)} %collective-permute-done.15), channel_id=1, source_target_pairs={{0,4},{4,0},{1,5},{5,1},{2,6},{6,2},{3,7},{7,3},{8,12},{12,8},{9,1... | collective-permute-start | bytes 241928 | tf_op jit(solution)/shard_map/ppermute | solution.py:52
  363.5 6.3 %collective-permute-start.17 = (bf16[3,70,192]{2,1,0:T(8,128)(2,1)S(1)}, bf16[3,70,192]{2,1,0:T(8,128)(2,1)S(1)}, u32[]{:S(2)}, u32[]{:S(2)}) collective-permute-start(bf16[3,70,192]{2,1,0:T(8,128)(2,1)S(1)} %collective-permute-done.16), channel_id=1, source_target_pairs={{0,8},{8,0},{1,9},{9,1},{2,10},{10,2},{3,11},{11,3},{4,12},{12,4},... | collective-permute-start | bytes 241928 | tf_op jit(solution)/shard_map/ppermute | solution.py:52
  (67 other events, 264.6 us)
where the time goes:
time: 467 us; the launch traced here: 462 us
  other arithmetic  172 us (37%)
  local copies, waits for them, and re-layouts  145 us (31%)
  matrix products  66.4 us (14%)
  waiting for transfers between devices  39.8 us (9%)
  starting transfers between devices  36 us (8%)
    reduce_sum x2, other arithmetic, layer_scale(): center = values - jnp.mean(values, axis=-1, keepdims=True)  148 us
    gather x1, local copies, waits for them, and re-layouts, body(): picked = band_flat[overlay_cell_index].astype(jnp.float32)  58.1 us
    reshape x3, local copies, waits for them, and re-layouts, to_windows(): tensor.reshape(row_total // WR, WR, column_total // WC, WC, HEADS, HD)  20.1 us
    transpose x3, local copies, waits for them, and re-layouts, to_windows(): return shaped.transpose(0, 2, 4, 1, 3, 5).reshape(-1, HEADS, WR * WC, HD)  18.9 us
    ppermute x5, starting transfers between devices, with_halo(): lax.ppermute(lax.slice_in_dim(block, 0, width, axis=dim), axis, backward)  18.2 us
    dot_general x2, matrix products, ocean_mlp(): return jnp.dot(active, down_weight, preferred_element_type=jnp.float32)  17.7 us
    ppermute x8, waiting for transfers between devices, swapped(): return lax.ppermute(block, axis, route)  14.9 us
    sub x1, matrix products, body(): probs = jax.nn.softmax(scores, axis=-1).astype(jnp.bfloat16)  11.8 us
  transfers between devices with their start and end apart: 19, of which 14 were waited for; matrix products, arithmetic and copies ran while one was open for 7% of the time, Pallas kernels for 0%

commit v1 on v0

v1 whole, which is shorter than its diff:
```python
import functools

import jax
import jax.numpy as jnp
from jax import lax
from jax.experimental import pallas as pl
from jax.experimental.pallas import tpu as pltpu
from jax.sharding import PartitionSpec as P

BF = jnp.bfloat16
F32 = jnp.float32
EPS = 1e-6
MESH = pl.DeviceIdType.MESH
CH = 4

CELLS = 512
def split(x):
    hi=x.astype(BF)
    return hi,(x-hi.astype(F32)).astype(BF)

def split_dot(x, ones):
    hi,lo=split(x)
    return jnp.dot(hi,ones,preferred_element_type=F32)+jnp.dot(lo,ones,preferred_element_type=F32)

def gelu(x):
    inner=x*(0.7978845608028654+0.035677408136300125*(x*x))
    h=0.5*x
    return h+h*jnp.tanh(inner)

NT = (((1,),(1,)),((),()))


def ocean_kernel(comm, flux_ref, index_ref, remap_ref, lift_ref, ocean_ref, wet_ref, taps_ref, gains_ref, up_ref, down_ref, head_ref, second_hbm, embed_ref,
                 updated_ref, out_ref, field_ref, next_ref, second_ref, table_ref, t_ref, wet_t, taps_pair, w_ref, x4_ref, a_ref, y_ref, n_ref, warm_ref,
                 rows_send, rows_recv, side_send, side_recv, corner_send, corner_recv, load_sem, flux_send, flux_recv, send_sem, recv_sem):
    load = pltpu.make_async_copy(second_hbm, second_ref, load_sem)
    load.start()
    if comm:
        lat = lax.axis_index("lat")
        lon = lax.axis_index("lon")
        lats = lax.axis_size("lat")
        lons = lax.axis_size("lon")
        top = lat == lats - 1
        bottom = lat == 0
        mirror = lons - 1 - lon
        up_id = (jnp.where(top, lat, lat + 1), jnp.where(top, mirror, lon))
        down_id = (jnp.where(bottom, lat, lat - 1), jnp.where(bottom, mirror, lon))
        west_id = (lat, lax.rem(lon + lons - 1, lons))
        east_id = (lat, lax.rem(lon + 1, lons))
        barrier = pltpu.get_barrier_semaphore()

        def greet(k, _):
            pl.semaphore_signal(barrier, inc=1, device_id=(lat, lax.rem(lon + k, lons)), device_id_type=MESH)
            return 0

        lax.fori_loop(1, lons, greet, 0)
        for other in (up_id, down_id):
            pl.semaphore_signal(barrier, inc=1, device_id=other, device_id_type=MESH)
        pl.semaphore_wait(barrier, lons + 1)
        up_slot = jnp.where(top, 0, 1)
        down_slot = jnp.where(bottom, 1, 0)

        def to_peer(k):
            return pltpu.make_async_remote_copy(
                src_ref=flux_ref, dst_ref=table_ref.at[lon], send_sem=flux_send.at[k], recv_sem=flux_recv.at[lon],
                device_id=(lat, lax.rem(lon + k, lons)), device_id_type=MESH,
            )

        def send(k, _):
            to_peer(k).start()
            return 0

        lax.fori_loop(1, lons, send, 0)
        table_ref[lon] = flux_ref[...]
    else:
        for d in range(16):
            table_ref[d] = flux_ref[...]

    wet = wet_ref[...].astype(F32)
    wet_t[...] = jnp.concatenate([wet, wet], axis=0).T

    def wet_from(row):
        return pltpu.roll(wet_t[...], 128 - row, axis=1)

    for blk in range(2):
        for g in range(3):
            piece = taps_ref[blk][:, 64 * g : 64 * g + 64]
            taps_pair[blk, g, 0:49] = jnp.concatenate([piece, piece], axis=1)
    sub = lax.broadcasted_iota(jnp.int32, (64, 128), 0)
    lane = lax.broadcasted_iota(jnp.int32, (64, 128), 1)
    low_diag = lane == sub
    high_diag = lane == sub + 64
    s2 = lax.broadcasted_iota(jnp.int32, (256, 256), 0) // 64
    l2 = lax.broadcasted_iota(jnp.int32, (256, 256), 1) // 64
    ones = jnp.where(s2 == l2, 1.0, 0.0).astype(BF)
    flip = lax.broadcasted_iota(jnp.int32, (64, 64), 0) + lax.broadcasted_iota(jnp.int32, (64, 64), 1)
    flip = jnp.where(flip == 63, 1.0, 0.0).astype(BF)

    def build_weights(blk):
        def build(b, _):
            for g in range(3):
                for d in range(3):
                    for q in range(4):
                        halves = []
                        for half in range(2):
                            a = 4 * (d - 1) + q - 2 * half + 3
                            value = jnp.zeros((64, 128), F32)
                            if 0 <= a - 1 < 7:
                                value = jnp.where(high_diag, taps_pair[blk, g, pl.ds(7 * (a - 1) + b, 1), :], value)
                            if 0 <= a < 7:
                                value = jnp.where(low_diag, taps_pair[blk, g, pl.ds(7 * a + b, 1), :], value)
                            halves.append(value.astype(BF))
                        row = pl.multiple_of(b * 256, 256) + (1792 * d + 64 * q)
                        w_ref[g, pl.ds(pl.multiple_of(row, 64), 64), :] = jnp.concatenate(halves, axis=1)
            return 0

        lax.fori_loop(0, 7, build, 0)

    build_weights(0)

    if comm:

        def receive(k, _):
            peer = lax.rem(lon + k, lons)
            pltpu.make_async_remote_copy(
                src_ref=flux_ref, dst_ref=table_ref.at[peer], send_sem=flux_send.at[k], recv_sem=flux_recv.at[peer],
                device_id=(lat, peer), device_id_type=MESH,
            ).wait_recv()
            return 0

        lax.fori_loop(1, lons, receive, 0)
    for h in range(4):
        t_ref[128 * h : 128 * h + 128, :] = table_ref[:, h].astype(F32).reshape(128, 256).astype(BF)
    ids = lax.broadcasted_iota(jnp.int32, (256, CELLS), 0)
    lift_hi, lift_lo = split(lift_ref[...])
    lift = jnp.concatenate([lift_hi, lift_hi, lift_lo], axis=0)

    def line(rows):
        return jnp.concatenate([rows[j : j + 1] for j in range(8)], axis=1)

    def force(i, _):
        total = jnp.zeros((8, CELLS), F32)
        for e in range(4):
            index = line(index_ref[e, pl.ds(pl.multiple_of(8 * i, 8), 8), :])
            lo = (index & 24) << 3 | ((index >> 9) & 7) << 3 | (index & 7)
            hi = jnp.broadcast_to((index >> 12) << 4 | ((index >> 5) & 15), (8, CELLS))
            hit = jnp.where(ids == lo, 1.0, 0.0).astype(BF)
            res = jnp.dot(t_ref[...], hit, preferred_element_type=F32)
            got = res[0:8]
            for k in range(1, 64):
                got = jnp.where(hi == k, res[8 * k : 8 * k + 8], got)
            total = total + got * line(remap_ref[e, pl.ds(pl.multiple_of(8 * i, 8), 8), :])
        high = total.astype(BF).astype(F32)
        spread = jnp.concatenate([high, total - high, high], axis=0).astype(BF)
        lifted = lax.dot_general(spread, lift, (((0,), (0,)), ((), ())), preferred_element_type=F32)
        here = wet_from(8 * i)
        for j in range(8):
            row = ocean_ref[8 * i + j].astype(F32) + lifted[64 * j : 64 * j + 64]
            field_ref[8 * i + j] = here[:, j : j + 1] * row
        return 0

    lax.fori_loop(0, 4096 // CELLS, force, 0)

    for blk in range(2):
        src = field_ref if blk == 0 else next_ref

        def remote(source, target, index, slot, device):
            return pltpu.make_async_remote_copy(
                src_ref=source, dst_ref=target, send_sem=send_sem.at[blk, index], recv_sem=recv_sem.at[blk, slot],
                device_id=device, device_id_type=MESH,
            )

        if comm:
            for k in range(3):
                turned = jnp.dot(flip, src[63 - k].astype(BF), preferred_element_type=F32)
                rows_send[blk, 0, k] = jnp.where(top, turned, src[61 + k]).astype(BF)
                rows_send[blk, 1, k] = src[k].astype(BF)
            early = lax.broadcasted_iota(jnp.int32, (32, 8, 192), 1) < 4
            west = src[:, 0:8, :].reshape(32, 2, 8, 192)
            east = src[:, 56:64, :].reshape(32, 2, 8, 192)
            side_send[blk, 0] = jnp.where(early, west[:, 0], pltpu.roll(west[:, 1], 4, axis=1)).astype(BF)
            side_send[blk, 1] = jnp.where(early, pltpu.roll(east[:, 0], 4, axis=1), east[:, 1]).astype(BF)
            copies = [
                remote(rows_send.at[blk, 0], rows_recv.at[blk, up_slot], 0, up_slot, up_id),
                remote(rows_send.at[blk, 1], rows_recv.at[blk, down_slot], 1, down_slot, down_id),
                remote(side_send.at[blk, 0], side_recv.at[blk, 1], 2, 3, west_id),
                remote(side_send.at[blk, 1], side_recv.at[blk, 0], 3, 2, east_id),
            ]
            for c in copies:
                c.start()
        if blk == 1:
            build_weights(1)
        if comm:
            remote(rows_send.at[blk, 0], rows_recv.at[blk, 0], 0, 0, up_id).wait_recv()
            remote(rows_send.at[blk, 0], rows_recv.at[blk, 1], 0, 1, up_id).wait_recv()
            for s in range(2):
                corner_send[blk, 0, s] = rows_recv[blk, s, :, 0:8, :]
                corner_send[blk, 1, s] = rows_recv[blk, s, :, 56:64, :]
            more = [
                remote(corner_send.at[blk, 0], corner_recv.at[blk, 1], 4, 5, west_id),
                remote(corner_send.at[blk, 1], corner_recv.at[blk, 0], 5, 4, east_id),
            ]
            for c in more:
                c.start()
            remote(side_send.at[blk, 0], side_recv.at[blk, 0], 2, 2, west_id).wait_recv()
            remote(side_send.at[blk, 0], side_recv.at[blk, 1], 2, 3, west_id).wait_recv()

        def place(i, rows):
            for g in range(3):
                x4_ref[g] = jnp.concatenate([r[:, 64 * g : 64 * g + 64] for r in rows], axis=1)
                for b in range(7):
                    a_ref[g, i, :, 256 * b : 256 * b + 256] = x4_ref[g, pl.ds(5 + b, 64), :].astype(BF)

        def group(i, _):
            rows = []
            for p in range(4):
                r = 4 * (i - 1) + p
                west = side_recv[blk, 0, 2 * (i - 1) + p // 2].astype(F32)
                east = side_recv[blk, 1, 2 * (i - 1) + p // 2].astype(F32)
                if p % 2 == 0:
                    west = pltpu.roll(west, 4, axis=0)
                else:
                    east = pltpu.roll(east, 4, axis=0)
                rows.append(jnp.concatenate([west, src[r], east], axis=0))
            place(i, rows)
            return 0

        lax.fori_loop(1, 17, group, 0)
        if comm:
            remote(corner_send.at[blk, 0], corner_recv.at[blk, 0], 4, 4, west_id).wait_recv()
            remote(corner_send.at[blk, 0], corner_recv.at[blk, 1], 4, 5, west_id).wait_recv()
        empty = jnp.zeros((80, 192), F32)

        def outer(s, k):
            pieces = [corner_recv[blk, 0, s, k], rows_recv[blk, s, k], corner_recv[blk, 1, s, k]]
            return jnp.concatenate([piece.astype(F32) for piece in pieces], axis=0)

        place(17, [outer(0, k) for k in range(3)] + [empty])
        souths = [outer(1, k) for k in range(3)]
        if comm:
            souths = [jnp.where(bottom, 0.0, s) for s in souths]
        place(0, [empty] + souths)

        def conv(ci):
            base = ci * CH
            for g in range(3):
                acc = None
                for d in range(3):
                    lhs = a_ref[g, pl.ds(base + d, CH)].reshape(CH * 64, 1792)
                    part = jnp.dot(lhs, w_ref[g, d * 1792 : (d + 1) * 1792, :], preferred_element_type=F32)
                    acc = part if acc is None else acc + part
                y_ref[g] = acc

        gains = [jnp.concatenate([gains_ref[blk : blk + 1, 64 * g : 64 * g + 64]] * 4, axis=1) for g in range(3)]

        def norm():
            mean = split_dot(y_ref[0] + y_ref[1] + y_ref[2], ones) * (1 / 192)
            cs = [y_ref[g] - mean for g in range(3)]
            var = split_dot(cs[0] * cs[0] + cs[1] * cs[1] + cs[2] * cs[2], ones) * (1 / 192)
            inv = lax.rsqrt(var + EPS)
            ns = [(cs[g] * inv * gains[g]).astype(BF) for g in range(3)]
            for p in range(4):
                n_ref[p] = jnp.concatenate([ns[g][:, 64 * p : 64 * p + 64] for g in range(3)], axis=1)

        def mlp(ci):
            base = ci * CH
            here = wet_from(16 * ci)
            temps = []
            for p in range(4):
                act = gelu(jnp.dot(n_ref[p], up_ref[blk], preferred_element_type=F32)).astype(BF)
                inc = lax.dot_general(act, down_ref[blk], NT, preferred_element_type=F32)
                news = []
                for j in range(CH):
                    r = 4 * (base + j) + p
                    new = src[r] + here[:, 4 * j + p : 4 * j + p + 1] * inc[64 * j : 64 * j + 64]
                    if blk == 1:
                        out_ref[r] = new.astype(BF)
                        news.append(new)
                    else:
                        next_ref[r] = new
                if blk == 1:
                    hi, lo = split(jnp.concatenate(news, axis=0))
                    head_hi, head_lo = split(jnp.broadcast_to(head_ref[...].reshape(1, 192), (128, 192)))
                    temps.append(
                        lax.dot_general(hi, head_hi, NT, preferred_element_type=F32)
                        + lax.dot_general(lo, head_hi, NT, preferred_element_type=F32)
                        + lax.dot_general(hi, head_lo, NT, preferred_element_type=F32)
                    )
            if blk == 1:
                for s in range(2):
                    warm_ref[0] = temps[2 * s] + temps[2 * s + 1]
                    for j in range(CH):
                        both = here[:, 4 * j + 2 * s : 4 * j + 2 * s + 1] + here[:, 4 * j + 2 * s + 1 : 4 * j + 2 * s + 2]
                        warm_ref[1, 64 * j : 64 * j + 64] = jnp.broadcast_to(both, (64, 128))
                    pair = lambda k: warm_ref[k, pl.ds(0, 128, stride=2), :] + warm_ref[k, pl.ds(1, 128, stride=2), :]
                    warmth = pair(0) / jnp.maximum(pair(1), 1.0)
                    for j in range(CH):
                        r = 2 * j + s
                        old = jnp.concatenate([second_ref[ci, 64 * c + 8 * r : 64 * c + 8 * r + 8, :] for c in range(4)], axis=0)
                        row = jnp.concatenate([warmth[32 * j : 32 * j + 32]] * 6, axis=1)
                        updated_ref[8 * ci + r] = (old + row * embed_ref[...].reshape(1, 768)).astype(BF)

        conv(0)
        if blk == 1:
            load.wait()

        def step(ci, _):
            norm()
            conv(ci)
            mlp(ci - 1)
            return 0

        lax.fori_loop(1, 16 // CH, step, 0)
        norm()
        mlp(16 // CH - 1)
        if comm:
            for c in copies + more:
                c.wait_send()
    if comm:

        def sent(k, _):
            to_peer(k).wait_send()
            return 0

        lax.fori_loop(1, lons, sent, 0)


def ocean_step(comm, fluxes, idx, remap, lift, ocean, wet, taps, gains, up, down, head, second, embed):
    vm = pl.BlockSpec(memory_space=pltpu.VMEM)
    far = pl.BlockSpec(memory_space=pl.ANY)
    width = second.shape[-1]
    dma = pltpu.SemaphoreType.DMA
    params = dict(collective_id=1, has_side_effects=True) if comm else {}
    return pl.pallas_call(
        functools.partial(ocean_kernel, comm),
        out_shape=[jax.ShapeDtypeStruct((32, 32, width), BF), jax.ShapeDtypeStruct((64, 64, 192), BF)],
        in_specs=[vm] * 11 + [far, vm],
        out_specs=[vm] * 2,
        scratch_shapes=[
            pltpu.VMEM((64, 64, 192), F32), pltpu.VMEM((64, 64, 192), F32), pltpu.VMEM((4, 256, width), F32),
            pltpu.VMEM((16, 4, 8, 256), BF), pltpu.VMEM((512, 256), BF), pltpu.VMEM((64, 128), F32), pltpu.VMEM((2, 3, 56, 128), F32),
            pltpu.VMEM((3, 21 * 256, 256), BF), pltpu.VMEM((3, 80, 256), F32), pltpu.VMEM((3, 18, 64, 1792), BF),
            pltpu.VMEM((3, CH * 64, 256), F32), pltpu.VMEM((4, CH * 64, 192), BF), pltpu.VMEM((2, CH * 64, 128), F32),
            pltpu.VMEM((2, 2, 3, 64, 192), BF), pltpu.VMEM((2, 2, 3, 64, 192), BF),
            pltpu.VMEM((2, 2, 32, 8, 192), BF), pltpu.VMEM((2, 2, 32, 8, 192), BF),
            pltpu.VMEM((2, 2, 2, 3, 8, 192), BF), pltpu.VMEM((2, 2, 2, 3, 8, 192), BF),
            dma, dma((16,)), dma((16,)), dma((2, 6)), dma((2, 6)),
        ],
        compiler_params=pltpu.CompilerParams(vmem_limit_bytes=60 * 2**20, **params),
        name="ocean",
        cost_estimate=pl.CostEstimate(flops=50 * 10**9, bytes_accessed=16 * 2**20, transcendentals=6 * 10**6),
    )(fluxes, idx, remap, lift, ocean, wet, taps, gains, up, down, head, second, embed)


def air_kernel(comm, x_ref, gain_attn_ref, gain_mlp_ref, qkv_hbm, out_hbm, up_hbm, down_hbm, head_ref, second_ref, flux_ref,
               qkv_w, out_w, up_w, down_w, normed, edge_send, edge_recv, qkv, beside, mixed, load_sem, send_sem, recv_sem):
    width = x_ref.shape[-1]
    loads = [
        pltpu.make_async_copy(source, target, load_sem.at[i])
        for i, (source, target) in enumerate(((qkv_hbm, qkv_w), (out_hbm, out_w), (up_hbm, up_w), (down_hbm, down_w)))
    ]
    for load in loads:
        load.start()
    if comm:
        lat = lax.axis_index("lat")
        lon = lax.axis_index("lon")
        count = lax.axis_size("lon")
        west_id = (lat, lax.rem(lon + count - 1, count))
        east_id = (lat, lax.rem(lon + 1, count))
        barrier = pltpu.get_barrier_semaphore()
        for other in (west_id, east_id):
            pl.semaphore_signal(barrier, inc=1, device_id=other, device_id_type=MESH)

    def cells(band, j):
        return x_ref[band, :, 8 * j : 8 * j + 8, :].astype(F32).reshape(64, width)

    def rms(values, gain):
        return (values * lax.rsqrt(jnp.mean(values * values, axis=1, keepdims=True) + EPS) * gain).astype(BF)

    for band in range(4):
        for side, j in ((0, 0), (1, 3)):
            block = rms(cells(band, j), gain_attn_ref[...].reshape(1, width))
            normed[band, j] = block
            edge_send[side, band] = block
    if comm:
        pl.semaphore_wait(barrier, 2)
        copies = [
            pltpu.make_async_remote_copy(
                src_ref=edge_send.at[side], dst_ref=edge_recv.at[1 - side], send_sem=send_sem.at[side],
                recv_sem=recv_sem.at[1 - side], device_id=device, device_id_type=MESH,
            )
            for side, device in ((0, west_id), (1, east_id))
        ]
        for copy in copies:
            copy.start()
    for band in range(4):
        for j in (1, 2):
            normed[band, j] = rms(cells(band, j), gain_attn_ref[...].reshape(1, width))
    loads[0].wait()

    def project(band, _):
        rows = normed[band].reshape(256, width)
        for part in range(3):
            lanes = slice(width * part, width * part + width)
            result = jnp.dot(rows, qkv_w[:, lanes], preferred_element_type=F32)
            if part == 0:
                result = result.astype(BF) * BF(0.125)
            qkv[band, :, :, lanes] = result.astype(BF).reshape(4, 64, width)
        return 0

    lax.fori_loop(0, 4, project, 0)
    if comm:
        for copy in copies:
            copy.wait_recv()

    def project_beside(side, _):
        rows = edge_recv[side].reshape(256, width)
        for part in range(2):
            lanes = slice(width * part, width * part + width)
            result = jnp.dot(rows, qkv_w[:, width * (part + 1) : width * (part + 2)], preferred_element_type=F32)
            beside[side, :, :, lanes] = result.astype(BF).reshape(4, 64, width)
        return 0

    lax.fori_loop(0, 2, project_beside, 0)
    even = lax.broadcasted_iota(jnp.int32, (128, 128), 1) < 64
    zero = jnp.zeros((128, 128), BF)
    tally = jnp.concatenate([jnp.where(even, 1.0, 0.0), jnp.where(even, 0.0, 1.0)], axis=0).astype(BF)

    def paired(block):
        return jnp.concatenate([jnp.where(even, block, zero), jnp.where(even, zero, block)], axis=0)

    def attention(band):
        for pair in range(6):
            q_lanes = slice(128 * pair, 128 * pair + 128)
            k_lanes = slice(width + 128 * pair, width + 128 * pair + 128)
            v_lanes = slice(2 * width + 128 * pair, 2 * width + 128 * pair + 128)
            hk_lanes, hv_lanes = q_lanes, k_lanes

            def window(keys, vals, query):
                keys = paired(keys)
                vals = jnp.concatenate([paired(vals), tally], axis=1)
                scores = lax.dot_general(query, keys, NT, preferred_element_type=F32)
                parts = [scores[:, :128], scores[:, 128:]]
                parts = [jnp.exp(s - jnp.max(s, axis=1, keepdims=True)).astype(BF) for s in parts]
                result = jnp.dot(jnp.concatenate(parts, axis=1), vals, preferred_element_type=F32)
                return (result[:, :128] / result[:, 128:]).astype(BF)

            def stack(*blocks):
                return jnp.concatenate(blocks, axis=0)

            mixed[0:64, q_lanes] = window(
                stack(beside[0, band, :, hk_lanes], qkv[band, 0, :, k_lanes]),
                stack(beside[0, band, :, hv_lanes], qkv[band, 0, :, v_lanes]),
                qkv[band, 0, :, q_lanes],
            )
            mixed[64:192, q_lanes] = window(
                stack(qkv[band, 1, :, k_lanes], qkv[band, 2, :, k_lanes]),
                stack(qkv[band, 1, :, v_lanes], qkv[band, 2, :, v_lanes]),
                stack(qkv[band, 1, :, q_lanes], qkv[band, 2, :, q_lanes]),
            )
            mixed[192:256, q_lanes] = window(
                stack(qkv[band, 3, :, k_lanes], beside[1, band, :, hk_lanes]),
                stack(qkv[band, 3, :, v_lanes], beside[1, band, :, hv_lanes]),
                qkv[band, 3, :, q_lanes],
            )

    def feed_forward(band):
        first = jnp.concatenate([cells(band, j) for j in range(4)], axis=0)
        first = first + jnp.dot(mixed[...], out_w[...], preferred_element_type=F32)
        rows = rms(first, gain_mlp_ref[...].reshape(1, width))
        total = first
        for part in range(4):
            lanes = slice(width * part, width * part + width)
            hidden = gelu(jnp.dot(rows, up_w[:, lanes], preferred_element_type=F32)).astype(BF)
            total = total + jnp.dot(hidden, down_w[lanes, :], preferred_element_type=F32)
        second_ref[band] = total
        flux_ref[band] = lax.dot_general(head_ref[...], total.astype(BF), NT, preferred_element_type=F32).astype(BF)

    attention(0)
    for load in loads[1:]:
        load.wait()

    def step(band, _):
        feed_forward(band - 1)
        attention(band)
        return 0

    lax.fori_loop(1, 4, step, 0)
    feed_forward(3)
    if comm:
        for copy in copies:
            copy.wait_send()


def atmosphere(comm, x, gain_attn, gain_mlp, qkv_w, out_w, up_w, down_w, flux_head):
    width = x.shape[-1]
    vm = pl.BlockSpec(memory_space=pltpu.VMEM)
    far = pl.BlockSpec(memory_space=pl.ANY)
    params = dict(collective_id=2, has_side_effects=True) if comm else {}
    return pl.pallas_call(
        functools.partial(air_kernel, comm),
        out_shape=[jax.ShapeDtypeStruct((4, 256, width), F32), jax.ShapeDtypeStruct((4, 8, 256), BF)],
        in_specs=[vm, vm, vm, far, far, far, far, vm],
        out_specs=[vm, vm],
        scratch_shapes=[
            pltpu.VMEM(qkv_w.shape, BF), pltpu.VMEM(out_w.shape, BF), pltpu.VMEM(up_w.shape, BF), pltpu.VMEM(down_w.shape, BF),
            pltpu.VMEM((4, 4, 64, width), BF),
            pltpu.VMEM((2, 4, 64, width), BF), pltpu.VMEM((2, 4, 64, width), BF),
            pltpu.VMEM((4, 4, 64, 3 * width), BF),
            pltpu.VMEM((2, 4, 64, 2 * width), BF),
            pltpu.VMEM((256, width), BF),
            pltpu.SemaphoreType.DMA((4,)), pltpu.SemaphoreType.DMA((2,)), pltpu.SemaphoreType.DMA((2,)),
        ],
        compiler_params=pltpu.CompilerParams(vmem_limit_bytes=56 * 2**20, **params),
        name="air",
        cost_estimate=pl.CostEstimate(flops=16 * 10**9, bytes_accessed=20 * 2**20, transcendentals=5 * 10**6),
    )(x.reshape(4, 8, 32, width), gain_attn, gain_mlp, qkv_w, out_w, up_w, down_w, jnp.swapaxes(flux_head, 0, 1))


def body(
    atmos_features,
    ocean_features,
    wet_cell_mask,
    overlay_cell_index,
    remap_weight,
    query_key_value_weight,
    attention_out_weight,
    feedforward_up_weight,
    feedforward_down_weight,
    attention_gain,
    feedforward_gain,
    flux_head_weight,
    surface_temp_embedding,
    forcing_lift_weight,
    depthwise_kernels,
    ocean_norm_gains,
    ocean_up_weights,
    ocean_down_weights,
    surface_temp_head,
):
    second, fluxes = atmosphere(
        True, atmos_features, attention_gain, feedforward_gain, query_key_value_weight, attention_out_weight,
        feedforward_up_weight, feedforward_down_weight, flux_head_weight,
    )
    updated, ocean_out = ocean_step(
        True, fluxes, overlay_cell_index, remap_weight, forcing_lift_weight, ocean_features, wet_cell_mask, depthwise_kernels,
        ocean_norm_gains, ocean_up_weights, jnp.swapaxes(ocean_down_weights, 1, 2), surface_temp_head, second,
        surface_temp_embedding,
    )
    return (updated, ocean_out)


def solution(mesh):
    cells = P("lat", "lon", None)
    in_specs = (cells, cells, P("lat", "lon"), P(None, "lat", "lon"), P(None, "lat", "lon")) + (P(),) * 14
    return jax.shard_map(body, mesh=mesh, in_specs=in_specs, out_specs=(cells, cells), check_vma=False)
```

time: 467 us -> 133 us (0.28)
  the two profiles are of different devices: /device:TPU:56 before, /device:TPU:1 now
where the time goes in v1:
time: 133 us
  Pallas kernels  126 us (95%)
  local copies, waits for them, and re-layouts  5.67 us (4%)
    pallas_call x1, Pallas kernels, ocean_step(): pl.pallas_call(functools.partial(ocean_kernel, comm), out_shape=[jax.Shap...  88.6 us
    pallas_call x1, Pallas kernels, atmosphere(): pl.pallas_call(functools.partial(air_kernel, comm), out_shape=[jax.ShapeD...  37.7 us
    unnamed x5, local copies, waits for them, and re-layouts  5.67 us

profile of v1, /device:TPU:1, one launch (start us, length us, event | category | flops | bytes accessed | tf_op | source)
XLA Modules:
  0.0 132.6 jit_solution(672014923460977443)
XLA Ops:
  0.6 1.5 %copy.21.taps_ref = f32[2,49,192]{2,1,0:T(8,128)} copy(f32[2,49,192]{2,0,1:T(2,128)} %param.33) | data formatting | bytes 150528 | tf_op args[14]
  2.2 37.7 %air.1 = (f32[4,256,768]{2,1,0:T(8,128)}, bf16[4,8,256]{2,1,0:T(8,128)(2,1)}) custom-call(bf16[4,8,32,768]{3,2,1,0:T(8,128)(2,1)} %bitcast.3, f32[768]{0:T(1024)} %gain_attn_ref.1, f32[768]{0:T(1024)} %gain_mlp_ref.1, bf16[768,2304]{1,0:T(8,128)(2,1)} %qkv_hbm.1, bf16[768,768]{1,0:T(8,128)(2,1)} %out_hbm.1, bf16[768,3072]{1,0:T(8,128)(2,1)} %up_hbm.1, ...), custom_call_target="tpu_custom_call" | custom-call | flops 16000000000 | bytes 20971520 | tf_op jit(solution)/shard_map/air/pallas_call | solution.py:500
  39.9 88.6 %ocean.1 = (bf16[32,32,768]{2,1,0:T(8,128)(2,1)}, bf16[64,64,192]{2,1,0:T(8,128)(2,1)}) custom-call(bf16[4,8,256]{2,1,0:T(8,128)(2,1)} %get-tuple-element.4.flux_ref, s32[4,64,64]{2,1,0:T(8,128)} %index_ref.1, f32[4,64,64]{2,1,0:T(8,128)} %remap_ref.1, f32[8,192]{1,0:T(8,128)} %lift_ref.1, bf16[64,64,192]{2,1,0:T(8,128)(2,1)} %ocean_ref.1, ...), custom_call_target="tpu_custom_call" | custom-call | flops 49999998976 | bytes 16777216 | tf_op jit(solution)/shard_map/ocean/pallas_call | solution.py:334
  128.5 0.0 copy-start
  128.5 2.8 %copy.24 = bf16[32,32,768]{2,1,0:T(8,128)(2,1)} copy(bf16[32,32,768]{2,1,0:T(8,128)(2,1)} %get-tuple-element.8) | data formatting | bytes 3145728
  131.3 0.0 copy-done
  131.3 1.3 copy.25
Async XLA Ops:
  128.5 2.8 %copy-start = (bf16[64,64,192]{2,1,0:T(8,128)(2,1)S(1)}, bf16[64,64,192]{2,1,0:T(8,128)(2,1)}, u32[]{:S(2)}) copy-start(bf16[64,64,192]{2,1,0:T(8,128)(2,1)} %get-tuple-element.9) | copy-start | bytes 4718596

commit v2 on v1

--- a/solution.py
+++ b/solution.py
@@ -30,9 +30,9 @@
 NT = (((1,),(1,)),((),()))
 
 
-def ocean_kernel(comm, flux_ref, index_ref, remap_ref, lift_ref, ocean_ref, wet_ref, taps_ref, gains_ref, up_ref, down_ref, head_ref, second_hbm, embed_ref,
-                 updated_ref, out_ref, field_ref, next_ref, second_ref, table_ref, t_ref, wet_t, taps_pair, w_ref, x4_ref, a_ref, y_ref, n_ref, warm_ref,
-                 rows_send, rows_recv, side_send, side_recv, corner_send, corner_recv, load_sem, flux_send, flux_recv, send_sem, recv_sem):
+def ocean_kernel(comm, table_ref, index_ref, remap_ref, lift_ref, ocean_ref, wet_ref, taps_ref, gains_ref, up_ref, down_ref, head_ref, second_hbm, embed_ref,
+                 updated_ref, out_ref, field_ref, next_ref, second_ref, t_ref, wet_t, taps_pair, w_ref, x4_ref, a_ref, y_ref, n_ref, warm_ref,
+                 rows_send, rows_recv, side_send, side_recv, corner_send, corner_recv, load_sem, send_sem, recv_sem):
     load = pltpu.make_async_copy(second_hbm, second_ref, load_sem)
     load.start()
     if comm:
@@ -49,32 +49,10 @@
         east_id = (lat, lax.rem(lon + 1, lons))
         barrier = pltpu.get_barrier_semaphore()
 
-        def greet(k, _):
-            pl.semaphore_signal(barrier, inc=1, device_id=(lat, lax.rem(lon + k, lons)), device_id_type=MESH)
-            return 0
-
-        lax.fori_loop(1, lons, greet, 0)
-        for other in (up_id, down_id):
+        for other in (up_id, down_id, west_id, east_id):
             pl.semaphore_signal(barrier, inc=1, device_id=other, device_id_type=MESH)
-        pl.semaphore_wait(barrier, lons + 1)
         up_slot = jnp.where(top, 0, 1)
         down_slot = jnp.where(bottom, 1, 0)
-
-        def to_peer(k):
-            return pltpu.make_async_remote_copy(
-                src_ref=flux_ref, dst_ref=table_ref.at[lon], send_sem=flux_send.at[k], recv_sem=flux_recv.at[lon],
-                device_id=(lat, lax.rem(lon + k, lons)), device_id_type=MESH,
-            )
-
-        def send(k, _):
-            to_peer(k).start()
-            return 0
-
-        lax.fori_loop(1, lons, send, 0)
-        table_ref[lon] = flux_ref[...]
-    else:
-        for d in range(16):
-            table_ref[d] = flux_ref[...]
 
     wet = wet_ref[...].astype(F32)
     wet_t[...] = jnp.concatenate([wet, wet], axis=0).T
@@ -116,19 +94,6 @@
 
         lax.fori_loop(0, 7, build, 0)
 
-    build_weights(0)
-
-    if comm:
-
-        def receive(k, _):
-            peer = lax.rem(lon + k, lons)
-            pltpu.make_async_remote_copy(
-                src_ref=flux_ref, dst_ref=table_ref.at[peer], send_sem=flux_send.at[k], recv_sem=flux_recv.at[peer],
-                device_id=(lat, peer), device_id_type=MESH,
-            ).wait_recv()
-            return 0
-
-        lax.fori_loop(1, lons, receive, 0)
     for h in range(4):
         t_ref[128 * h : 128 * h + 128, :] = table_ref[:, h].astype(F32).reshape(128, 256).astype(BF)
     ids = lax.broadcasted_iota(jnp.int32, (256, CELLS), 0)
@@ -159,51 +124,86 @@
             field_ref[8 * i + j] = here[:, j : j + 1] * row
         return 0
 
-    lax.fori_loop(0, 4096 // CELLS, force, 0)
+    def remote(blk, source, target, index, slot, device):
+        return pltpu.make_async_remote_copy(
+            src_ref=source, dst_ref=target, send_sem=send_sem.at[blk, index], recv_sem=recv_sem.at[blk, slot],
+            device_id=device, device_id_type=MESH,
+        )
+
+    def down_copy(blk):
+        return remote(blk, rows_send.at[blk, 1], rows_recv.at[blk, down_slot], 1, down_slot, down_id)
+
+    def up_copy(blk):
+        return remote(blk, rows_send.at[blk, 0], rows_recv.at[blk, up_slot], 0, up_slot, up_id)
+
+    def corner_copies(blk):
+        return [
+            remote(blk, corner_send.at[blk, 0], corner_recv.at[blk, 1], 2, 3, west_id),
+            remote(blk, corner_send.at[blk, 1], corner_recv.at[blk, 0], 3, 2, east_id),
+        ]
+
+    def side_copies(blk, ci):
+        part = pl.ds(8 * ci, 8)
+        return [
+            remote(blk, side_send.at[blk, 0, part], side_recv.at[blk, 1, part], 4 + ci, 8 + ci, west_id),
+            remote(blk, side_send.at[blk, 1, part], side_recv.at[blk, 0, part], 8 + ci, 4 + ci, east_id),
+        ]
+
+    def ship(blk, src, ci):
+        early = lax.broadcasted_iota(jnp.int32, (8, 8, 192), 1) < 4
+        west = src[pl.ds(16 * ci, 16), 0:8, :].reshape(8, 2, 8, 192)
+        east = src[pl.ds(16 * ci, 16), 56:64, :].reshape(8, 2, 8, 192)
+        part = pl.ds(8 * ci, 8)
+        side_send[blk, 0, part] = jnp.where(early, west[:, 0], pltpu.roll(west[:, 1], 4, axis=1)).astype(BF)
+        side_send[blk, 1, part] = jnp.where(early, pltpu.roll(east[:, 0], 4, axis=1), east[:, 1]).astype(BF)
+        for c in side_copies(blk, ci):
+            c.start()
+
+    def ship_down(blk, src):
+        for k in range(3):
+            rows_send[blk, 1, k] = src[k].astype(BF)
+        down_copy(blk).start()
+
+    def ship_up(blk, src):
+        for k in range(3):
+            turned = jnp.dot(flip, src[63 - k].astype(BF), preferred_element_type=F32)
+            rows_send[blk, 0, k] = jnp.where(top, turned, src[61 + k]).astype(BF)
+        up_copy(blk).start()
+
+    if comm:
+        pl.semaphore_wait(barrier, 4)
+
+    def force_part(ci, _):
+        force(2 * ci, 0)
+        force(2 * ci + 1, 0)
+        if comm:
+            ship(0, field_ref, ci)
+
+            @pl.when(ci == 0)
+            def _():
+                ship_down(0, field_ref)
+
+        return 0
+
+    lax.fori_loop(0, 4, force_part, 0)
+    if comm:
+        ship_up(0, field_ref)
 
     for blk in range(2):
         src = field_ref if blk == 0 else next_ref
 
-        def remote(source, target, index, slot, device):
-            return pltpu.make_async_remote_copy(
-                src_ref=source, dst_ref=target, send_sem=send_sem.at[blk, index], recv_sem=recv_sem.at[blk, slot],
-                device_id=device, device_id_type=MESH,
-            )
-
+        build_weights(blk)
         if comm:
-            for k in range(3):
-                turned = jnp.dot(flip, src[63 - k].astype(BF), preferred_element_type=F32)
-                rows_send[blk, 0, k] = jnp.where(top, turned, src[61 + k]).astype(BF)
-                rows_send[blk, 1, k] = src[k].astype(BF)
-            early = lax.broadcasted_iota(jnp.int32, (32, 8, 192), 1) < 4
-            west = src[:, 0:8, :].reshape(32, 2, 8, 192)
-            east = src[:, 56:64, :].reshape(32, 2, 8, 192)
-            side_send[blk, 0] = jnp.where(early, west[:, 0], pltpu.roll(west[:, 1], 4, axis=1)).astype(BF)
-            side_send[blk, 1] = jnp.where(early, pltpu.roll(east[:, 0], 4, axis=1), east[:, 1]).astype(BF)
-            copies = [
-                remote(rows_send.at[blk, 0], rows_recv.at[blk, up_slot], 0, up_slot, up_id),
-                remote(rows_send.at[blk, 1], rows_recv.at[blk, down_slot], 1, down_slot, down_id),
-                remote(side_send.at[blk, 0], side_recv.at[blk, 1], 2, 3, west_id),
-                remote(side_send.at[blk, 1], side_recv.at[blk, 0], 3, 2, east_id),
-            ]
-            for c in copies:
-                c.start()
-        if blk == 1:
-            build_weights(1)
-        if comm:
-            remote(rows_send.at[blk, 0], rows_recv.at[blk, 0], 0, 0, up_id).wait_recv()
-            remote(rows_send.at[blk, 0], rows_recv.at[blk, 1], 0, 1, up_id).wait_recv()
+            remote(blk, rows_send.at[blk, 0], rows_recv.at[blk, 0], 0, 0, up_id).wait_recv()
+            remote(blk, rows_send.at[blk, 0], rows_recv.at[blk, 1], 0, 1, up_id).wait_recv()
             for s in range(2):
                 corner_send[blk, 0, s] = rows_recv[blk, s, :, 0:8, :]
                 corner_send[blk, 1, s] = rows_recv[blk, s, :, 56:64, :]
-            more = [
-                remote(corner_send.at[blk, 0], corner_recv.at[blk, 1], 4, 5, west_id),
-                remote(corner_send.at[blk, 1], corner_recv.at[blk, 0], 5, 4, east_id),
-            ]
-            for c in more:
+            for c in corner_copies(blk):
                 c.start()
-            remote(side_send.at[blk, 0], side_recv.at[blk, 0], 2, 2, west_id).wait_recv()
-            remote(side_send.at[blk, 0], side_recv.at[blk, 1], 2, 3, west_id).wait_recv()
+            for ci in range(4):
+                for c in side_copies(blk, ci):
+                    c.wait_recv()
 
         def place(i, rows):
             for g in range(3):
@@ -227,8 +227,8 @@
 
         lax.fori_loop(1, 17, group, 0)
         if comm:
-            remote(corner_send.at[blk, 0], corner_recv.at[blk, 0], 4, 4, west_id).wait_recv()
-            remote(corner_send.at[blk, 0], corner_recv.at[blk, 1], 4, 5, west_id).wait_recv()
+            for c in corner_copies(blk):
+                c.wait_recv()
         empty = jnp.zeros((80, 192), F32)
 
         def outer(s, k):
@@ -308,24 +308,31 @@
             norm()
             conv(ci)
             mlp(ci - 1)
+            if comm and blk == 0:
+                ship(1, next_ref, ci - 1)
+
+                @pl.when(ci == 1)
+                def _():
+                    ship_down(1, next_ref)
+
             return 0
 
         lax.fori_loop(1, 16 // CH, step, 0)
         norm()
         mlp(16 // CH - 1)
-        if comm:
-            for c in copies + more:
+        if comm and blk == 0:
+            ship(1, next_ref, 16 // CH - 1)
+            ship_up(1, next_ref)
+    if comm:
+        for blk in range(2):
+            for c in [up_copy(blk), down_copy(blk), *corner_copies(blk)]:
                 c.wait_send()
-    if comm:
-
-        def sent(k, _):
-            to_peer(k).wait_send()
-            return 0
-
-        lax.fori_loop(1, lons, sent, 0)
-
-
-def ocean_step(comm, fluxes, idx, remap, lift, ocean, wet, taps, gains, up, down, head, second, embed):
+            for ci in range(4):
+                for c in side_copies(blk, ci):
+                    c.wait_send()
+
+
+def ocean_step(comm, table, idx, remap, lift, ocean, wet, taps, gains, up, down, head, second, embed):
     vm = pl.BlockSpec(memory_space=pltpu.VMEM)
     far = pl.BlockSpec(memory_space=pl.ANY)
     width = second.shape[-1]
@@ -338,22 +345,22 @@
         out_specs=[vm] * 2,
         scratch_shapes=[
             pltpu.VMEM((64, 64, 192), F32), pltpu.VMEM((64, 64, 192), F32), pltpu.VMEM((4, 256, width), F32),
-            pltpu.VMEM((16, 4, 8, 256), BF), pltpu.VMEM((512, 256), BF), pltpu.VMEM((64, 128), F32), pltpu.VMEM((2, 3, 56, 128), F32),
+            pltpu.VMEM((512, 256), BF), pltpu.VMEM((64, 128), F32), pltpu.VMEM((2, 3, 56, 128), F32),
             pltpu.VMEM((3, 21 * 256, 256), BF), pltpu.VMEM((3, 80, 256), F32), pltpu.VMEM((3, 18, 64, 1792), BF),
             pltpu.VMEM((3, CH * 64, 256), F32), pltpu.VMEM((4, CH * 64, 192), BF), pltpu.VMEM((2, CH * 64, 128), F32),
             pltpu.VMEM((2, 2, 3, 64, 192), BF), pltpu.VMEM((2, 2, 3, 64, 192), BF),
             pltpu.VMEM((2, 2, 32, 8, 192), BF), pltpu.VMEM((2, 2, 32, 8, 192), BF),
             pltpu.VMEM((2, 2, 2, 3, 8, 192), BF), pltpu.VMEM((2, 2, 2, 3, 8, 192), BF),
-            dma, dma((16,)), dma((16,)), dma((2, 6)), dma((2, 6)),
+            dma, dma((2, 12)), dma((2, 12)),
         ],
         compiler_params=pltpu.CompilerParams(vmem_limit_bytes=60 * 2**20, **params),
         name="ocean",
         cost_estimate=pl.CostEstimate(flops=50 * 10**9, bytes_accessed=16 * 2**20, transcendentals=6 * 10**6),
-    )(fluxes, idx, remap, lift, ocean, wet, taps, gains, up, down, head, second, embed)
-
-
-def air_kernel(comm, x_ref, gain_attn_ref, gain_mlp_ref, qkv_hbm, out_hbm, up_hbm, down_hbm, head_ref, second_ref, flux_ref,
-               qkv_w, out_w, up_w, down_w, normed, edge_send, edge_recv, qkv, beside, mixed, load_sem, send_sem, recv_sem):
+    )(table, idx, remap, lift, ocean, wet, taps, gains, up, down, head, second, embed)
+
+
+def air_kernel(comm, x_ref, gain_attn_ref, gain_mlp_ref, qkv_hbm, out_hbm, up_hbm, down_hbm, head_ref, second_ref, table_ref,
+               qkv_w, out_w, up_w, down_w, normed, edge_send, edge_recv, qkv, beside, mixed, flux_ref, load_sem, send_sem, recv_sem, flux_send, flux_recv):
     width = x_ref.shape[-1]
     loads = [
         pltpu.make_async_copy(source, target, load_sem.at[i])
@@ -368,8 +375,34 @@
         west_id = (lat, lax.rem(lon + count - 1, count))
         east_id = (lat, lax.rem(lon + 1, count))
         barrier = pltpu.get_barrier_semaphore()
-        for other in (west_id, east_id):
-            pl.semaphore_signal(barrier, inc=1, device_id=other, device_id_type=MESH)
+
+        def greet(k, _):
+            pl.semaphore_signal(barrier, inc=1, device_id=(lat, lax.rem(lon + k, count)), device_id_type=MESH)
+            return 0
+
+        lax.fori_loop(1, count, greet, 0)
+
+        def flux_copy(part, k):
+            bands = (slice(0, 3), slice(3, 4))[part]
+            return pltpu.make_async_remote_copy(
+                src_ref=flux_ref.at[bands], dst_ref=table_ref.at[lon, bands], send_sem=flux_send.at[part, k],
+                recv_sem=flux_recv.at[part, lon], device_id=(lat, lax.rem(lon + k, count)), device_id_type=MESH,
+            )
+
+        def flux_arrival(part, k):
+            bands = (slice(0, 3), slice(3, 4))[part]
+            peer = lax.rem(lon + k, count)
+            return pltpu.make_async_remote_copy(
+                src_ref=flux_ref.at[bands], dst_ref=table_ref.at[peer, bands], send_sem=flux_send.at[part, k],
+                recv_sem=flux_recv.at[part, peer], device_id=(lat, peer), device_id_type=MESH,
+            )
+
+        def over_peers(part, act):
+            def one(k, _):
+                act(part, k)
+                return 0
+
+            lax.fori_loop(1, count, one, 0)
 
     def cells(band, j):
         return x_ref[band, :, 8 * j : 8 * j + 8, :].astype(F32).reshape(64, width)
@@ -383,7 +416,7 @@
             normed[band, j] = block
             edge_send[side, band] = block
     if comm:
-        pl.semaphore_wait(barrier, 2)
+        pl.semaphore_wait(barrier, count - 1)
         copies = [
             pltpu.make_async_remote_copy(
                 src_ref=edge_send.at[side], dst_ref=edge_recv.at[1 - side], send_sem=send_sem.at[side],
@@ -486,10 +519,19 @@
         return 0
 
     lax.fori_loop(1, 4, step, 0)
+    if comm:
+        over_peers(0, lambda part, k: flux_copy(part, k).start())
     feed_forward(3)
     if comm:
+        over_peers(1, lambda part, k: flux_copy(part, k).start())
+        table_ref[lon] = flux_ref[...]
         for copy in copies:
             copy.wait_send()
+        for part in range(2):
+            over_peers(part, lambda part, k: flux_arrival(part, k).wait_recv())
+            over_peers(part, lambda part, k: flux_copy(part, k).wait_send())
+    else:
+        table_ref[0] = flux_ref[...]
 
 
 def atmosphere(comm, x, gain_attn, gain_mlp, qkv_w, out_w, up_w, down_w, flux_head):
@@ -499,7 +541,7 @@
     params = dict(collective_id=2, has_side_effects=True) if comm else {}
     return pl.pallas_call(
         functools.partial(air_kernel, comm),
-        out_shape=[jax.ShapeDtypeStruct((4, 256, width), F32), jax.ShapeDtypeStruct((4, 8, 256), BF)],
+        out_shape=[jax.ShapeDtypeStruct((4, 256, width), F32), jax.ShapeDtypeStruct((16, 4, 8, 256), BF)],
         in_specs=[vm, vm, vm, far, far, far, far, vm],
         out_specs=[vm, vm],
         scratch_shapes=[
@@ -508,8 +550,9 @@
             pltpu.VMEM((2, 4, 64, width), BF), pltpu.VMEM((2, 4, 64, width), BF),
             pltpu.VMEM((4, 4, 64, 3 * width), BF),
             pltpu.VMEM((2, 4, 64, 2 * width), BF),
-            pltpu.VMEM((256, width), BF),
+            pltpu.VMEM((256, width), BF), pltpu.VMEM((4, 8, 256), BF),
             pltpu.SemaphoreType.DMA((4,)), pltpu.SemaphoreType.DMA((2,)), pltpu.SemaphoreType.DMA((2,)),
+            pltpu.SemaphoreType.DMA((2, 16)), pltpu.SemaphoreType.DMA((2, 16)),
         ],
         compiler_params=pltpu.CompilerParams(vmem_limit_bytes=56 * 2**20, **params),
         name="air",
@@ -538,12 +581,12 @@
     ocean_down_weights,
     surface_temp_head,
 ):
-    second, fluxes = atmosphere(
+    second, table = atmosphere(
         True, atmos_features, attention_gain, feedforward_gain, query_key_value_weight, attention_out_weight,
         feedforward_up_weight, feedforward_down_weight, flux_head_weight,
     )
     updated, ocean_out = ocean_step(
-        True, fluxes, overlay_cell_index, remap_weight, forcing_lift_weight, ocean_features, wet_cell_mask, depthwise_kernels,
+        True, table, overlay_cell_index, remap_weight, forcing_lift_weight, ocean_features, wet_cell_mask, depthwise_kernels,
         ocean_norm_gains, ocean_up_weights, jnp.swapaxes(ocean_down_weights, 1, 2), surface_temp_head, second,
         surface_temp_embedding,
     )

time: 133 us -> 123 us (0.925)
  the two profiles are of different devices: /device:TPU:1 before, /device:TPU:56 now
where the time goes in v2:
time: 123 us
  Pallas kernels  117 us (95%)
  local copies, waits for them, and re-layouts  5.67 us (5%)
    pallas_call x1, Pallas kernels, ocean_step(): pl.pallas_call(functools.partial(ocean_kernel, comm), out_shape=[jax.Shap...  72.1 us
    pallas_call x1, Pallas kernels, atmosphere(): pl.pallas_call(functools.partial(air_kernel, comm), out_shape=[jax.ShapeD...  44.5 us
    unnamed x5, local copies, waits for them, and re-layouts  5.67 us

profile of v2, /device:TPU:56, one launch (start us, length us, event | category | flops | bytes accessed | tf_op | source)
XLA Modules:
  0.0 122.9 jit_solution(14972317439617078432)
XLA Ops:
  0.6 1.5 %copy.21.taps_ref = f32[2,49,192]{2,1,0:T(8,128)} copy(f32[2,49,192]{2,0,1:T(2,128)} %param.33) | data formatting | bytes 150528 | tf_op args[14]
  2.2 44.5 %air.1 = (f32[4,256,768]{2,1,0:T(8,128)}, bf16[16,4,8,256]{3,2,1,0:T(8,128)(2,1)}) custom-call(bf16[4,8,32,768]{3,2,1,0:T(8,128)(2,1)} %bitcast.3, f32[768]{0:T(1024)} %gain_attn_ref.1, f32[768]{0:T(1024)} %gain_mlp_ref.1, bf16[768,2304]{1,0:T(8,128)(2,1)} %qkv_hbm.1, bf16[768,768]{1,0:T(8,128)(2,1)} %out_hbm.1, bf16[768,3072]{1,0:T(8,128)(2,1)} %up_hbm.1, ...), custom_call_target="tpu_custom_call" | custom-call | flops 16000000000 | bytes 20971520 | tf_op jit(solution)/shard_map/air/pallas_call | solution.py:542
  46.7 72.1 %ocean.1 = (bf16[32,32,768]{2,1,0:T(8,128)(2,1)}, bf16[64,64,192]{2,1,0:T(8,128)(2,1)}) custom-call(bf16[16,4,8,256]{3,2,1,0:T(8,128)(2,1)} %get-tuple-element.4.table_ref, s32[4,64,64]{2,1,0:T(8,128)} %index_ref.1, f32[4,64,64]{2,1,0:T(8,128)} %remap_ref.1, f32[8,192]{1,0:T(8,128)} %lift_ref.1, bf16[64,64,192]{2,1,0:T(8,128)(2,1)} %ocean_ref.1, ...), custom_call_target="tpu_custom_call" | custom-call | flops 49999998976 | bytes 16777216 | tf_op jit(solution)/shard_map/ocean/pallas_call | solution.py:341
  118.7 0.0 copy-start
  118.7 2.8 %copy.24 = bf16[32,32,768]{2,1,0:T(8,128)(2,1)} copy(bf16[32,32,768]{2,1,0:T(8,128)(2,1)} %get-tuple-element.8) | data formatting | bytes 3145728
  121.5 0.0 copy-done
  121.5 1.3 %copy.25 = bf16[64,64,192]{2,1,0:T(8,128)(2,1)} copy(bf16[64,64,192]{2,1,0:T(8,128)(2,1)S(1)} %copy-done) | data formatting | bytes 3145728
Async XLA Ops:
  118.7 2.8 %copy-start = (bf16[64,64,192]{2,1,0:T(8,128)(2,1)S(1)}, bf16[64,64,192]{2,1,0:T(8,128)(2,1)}, u32[]{:S(2)}) copy-start(bf16[64,64,192]{2,1,0:T(8,128)(2,1)} %get-tuple-element.9) | copy-start | bytes 4718596

commit v3 on v2

--- a/solution.py
+++ b/solution.py
@@ -62,7 +62,7 @@
 
     for blk in range(2):
         for g in range(3):
-            piece = taps_ref[blk][:, 64 * g : 64 * g + 64]
+            piece = taps_ref[:, blk, 64 * g : 64 * g + 64]
             taps_pair[blk, g, 0:49] = jnp.concatenate([piece, piece], axis=1)
     sub = lax.broadcasted_iota(jnp.int32, (64, 128), 0)
     lane = lax.broadcasted_iota(jnp.int32, (64, 128), 1)
@@ -356,7 +356,7 @@
         compiler_params=pltpu.CompilerParams(vmem_limit_bytes=60 * 2**20, **params),
         name="ocean",
         cost_estimate=pl.CostEstimate(flops=50 * 10**9, bytes_accessed=16 * 2**20, transcendentals=6 * 10**6),
-    )(table, idx, remap, lift, ocean, wet, taps, gains, up, down, head, second, embed)
+    )(table, idx, remap, lift, ocean, wet, jnp.swapaxes(taps, 0, 1), gains, up, down, head, second, embed)
 
 
 def air_kernel(comm, x_ref, gain_attn_ref, gain_mlp_ref, qkv_hbm, out_hbm, up_hbm, down_hbm, head_ref, second_ref, table_ref,
@@ -442,19 +442,6 @@
         return 0
 
     lax.fori_loop(0, 4, project, 0)
-    if comm:
-        for copy in copies:
-            copy.wait_recv()
-
-    def project_beside(side, _):
-        rows = edge_recv[side].reshape(256, width)
-        for part in range(2):
-            lanes = slice(width * part, width * part + width)
-            result = jnp.dot(rows, qkv_w[:, width * (part + 1) : width * (part + 2)], preferred_element_type=F32)
-            beside[side, :, :, lanes] = result.astype(BF).reshape(4, 64, width)
-        return 0
-
-    lax.fori_loop(0, 2, project_beside, 0)
     even = lax.broadcasted_iota(jnp.int32, (128, 128), 1) < 64
     zero = jnp.zeros((128, 128), BF)
     tally = jnp.concatenate([jnp.where(even, 1.0, 0.0), jnp.where(even, 0.0, 1.0)], axis=0).astype(BF)
@@ -462,44 +449,41 @@
     def paired(block):
         return jnp.concatenate([jnp.where(even, block, zero), jnp.where(even, zero, block)], axis=0)
 
-    def attention(band):
+    def window(keys, vals, query):
+        keys = paired(stack(*keys))
+        vals = jnp.concatenate([paired(stack(*vals)), tally], axis=1)
+        scores = lax.dot_general(stack(*query), keys, NT, preferred_element_type=F32)
+        parts = [scores[:, :128], scores[:, 128:]]
+        parts = [jnp.exp(s - jnp.max(s, axis=1, keepdims=True)).astype(BF) for s in parts]
+        result = jnp.dot(jnp.concatenate(parts, axis=1), vals, preferred_element_type=F32)
+        return (result[:, :128] / result[:, 128:]).astype(BF)
+
+    def stack(*blocks):
+        return jnp.concatenate(blocks, axis=0)
+
+    def pair_lanes(pair):
+        return [slice(width * part + 128 * pair, width * part + 128 * pair + 128) for part in range(3)]
+
+    def middle(band):
         for pair in range(6):
-            q_lanes = slice(128 * pair, 128 * pair + 128)
-            k_lanes = slice(width + 128 * pair, width + 128 * pair + 128)
-            v_lanes = slice(2 * width + 128 * pair, 2 * width + 128 * pair + 128)
-            hk_lanes, hv_lanes = q_lanes, k_lanes
-
-            def window(keys, vals, query):
-                keys = paired(keys)
-                vals = jnp.concatenate([paired(vals), tally], axis=1)
-                scores = lax.dot_general(query, keys, NT, preferred_element_type=F32)
-                parts = [scores[:, :128], scores[:, 128:]]
-                parts = [jnp.exp(s - jnp.max(s, axis=1, keepdims=True)).astype(BF) for s in parts]
-                result = jnp.dot(jnp.concatenate(parts, axis=1), vals, preferred_element_type=F32)
-                return (result[:, :128] / result[:, 128:]).astype(BF)
-
-            def stack(*blocks):
-                return jnp.concatenate(blocks, axis=0)
-
-            mixed[0:64, q_lanes] = window(
-                stack(beside[0, band, :, hk_lanes], qkv[band, 0, :, k_lanes]),
-                stack(beside[0, band, :, hv_lanes], qkv[band, 0, :, v_lanes]),
-                qkv[band, 0, :, q_lanes],
+            q, k, v = pair_lanes(pair)
+            mixed[band, 64:192, q] = window(
+                [qkv[band, 1, :, k], qkv[band, 2, :, k]], [qkv[band, 1, :, v], qkv[band, 2, :, v]], [qkv[band, 1, :, q], qkv[band, 2, :, q]]
             )
-            mixed[64:192, q_lanes] = window(
-                stack(qkv[band, 1, :, k_lanes], qkv[band, 2, :, k_lanes]),
-                stack(qkv[band, 1, :, v_lanes], qkv[band, 2, :, v_lanes]),
-                stack(qkv[band, 1, :, q_lanes], qkv[band, 2, :, q_lanes]),
+
+    def edges(band):
+        for pair in range(6):
+            q, k, v = pair_lanes(pair)
+            mixed[band, 0:64, q] = window(
+                [beside[0, band, :, q], qkv[band, 0, :, k]], [beside[0, band, :, k], qkv[band, 0, :, v]], [qkv[band, 0, :, q]]
             )
-            mixed[192:256, q_lanes] = window(
-                stack(qkv[band, 3, :, k_lanes], beside[1, band, :, hk_lanes]),
-                stack(qkv[band, 3, :, v_lanes], beside[1, band, :, hv_lanes]),
-                qkv[band, 3, :, q_lanes],
+            mixed[band, 192:256, q] = window(
+                [qkv[band, 3, :, k], beside[1, band, :, q]], [qkv[band, 3, :, v], beside[1, band, :, k]], [qkv[band, 3, :, q]]
             )
 
     def feed_forward(band):
         first = jnp.concatenate([cells(band, j) for j in range(4)], axis=0)
-        first = first + jnp.dot(mixed[...], out_w[...], preferred_element_type=F32)
+        first = first + jnp.dot(mixed[band], out_w[...], preferred_element_type=F32)
         rows = rms(first, gain_mlp_ref[...].reshape(1, width))
         total = first
         for part in range(4):
@@ -509,13 +493,31 @@
         second_ref[band] = total
         flux_ref[band] = lax.dot_general(head_ref[...], total.astype(BF), NT, preferred_element_type=F32).astype(BF)
 
-    attention(0)
+    def middle_step(band, _):
+        middle(band)
+        return 0
+
+    lax.fori_loop(0, 4, middle_step, 0)
+    if comm:
+        for copy in copies:
+            copy.wait_recv()
+
+    def project_beside(side, _):
+        rows = edge_recv[side].reshape(256, width)
+        for part in range(2):
+            lanes = slice(width * part, width * part + width)
+            result = jnp.dot(rows, qkv_w[:, width * (part + 1) : width * (part + 2)], preferred_element_type=F32)
+            beside[side, :, :, lanes] = result.astype(BF).reshape(4, 64, width)
+        return 0
+
+    lax.fori_loop(0, 2, project_beside, 0)
+    edges(0)
     for load in loads[1:]:
         load.wait()
 
     def step(band, _):
         feed_forward(band - 1)
-        attention(band)
+        edges(band)
         return 0
 
     lax.fori_loop(1, 4, step, 0)
@@ -550,7 +552,7 @@
             pltpu.VMEM((2, 4, 64, width), BF), pltpu.VMEM((2, 4, 64, width), BF),
             pltpu.VMEM((4, 4, 64, 3 * width), BF),
             pltpu.VMEM((2, 4, 64, 2 * width), BF),
-            pltpu.VMEM((256, width), BF), pltpu.VMEM((4, 8, 256), BF),
+            pltpu.VMEM((4, 256, width), BF), pltpu.VMEM((4, 8, 256), BF),
             pltpu.SemaphoreType.DMA((4,)), pltpu.SemaphoreType.DMA((2,)), pltpu.SemaphoreType.DMA((2,)),
             pltpu.SemaphoreType.DMA((2, 16)), pltpu.SemaphoreType.DMA((2, 16)),
         ],

time: 123 us -> 121 us (0.984)
  local copies, waits for them, and re-layouts: 5.67 us -> 4.12 us
    unnamed x5 -> x4, local copies, waits for them, and re-layouts: 5.67 us -> 4.12 us
where the time goes in v3:
time: 121 us; the launch traced here: 120 us
  Pallas kernels  116 us (96%)
  local copies, waits for them, and re-layouts  4.12 us (3%)
    pallas_call x1, Pallas kernels, ocean_step(): pl.pallas_call(functools.partial(ocean_kernel, comm), out_shape=[jax.Shap...  72.2 us
    pallas_call x1, Pallas kernels, atmosphere(): pl.pallas_call(functools.partial(air_kernel, comm), out_shape=[jax.ShapeD...  43.5 us
    unnamed x4, local copies, waits for them, and re-layouts  4.12 us

profile of v3, /device:TPU:56, one launch (start us, length us, event | category | flops | bytes accessed | tf_op | source)
XLA Modules:
  0.0 120.4 jit_solution(11307392794379898835)
XLA Ops:
  0.6 43.5 %air.1 = (f32[4,256,768]{2,1,0:T(8,128)}, bf16[16,4,8,256]{3,2,1,0:T(8,128)(2,1)}) custom-call(bf16[4,8,32,768]{3,2,1,0:T(8,128)(2,1)} %bitcast.4, f32[768]{0:T(1024)} %gain_attn_ref.1, f32[768]{0:T(1024)} %gain_mlp_ref.1, bf16[768,2304]{1,0:T(8,128)(2,1)} %qkv_hbm.1, bf16[768,768]{1,0:T(8,128)(2,1)} %out_hbm.1, bf16[768,3072]{1,0:T(8,128)(2,1)} %up_hbm.1, ...), custom_call_target="tpu_custom_call" | custom-call | flops 16000000000 | bytes 20971520 | tf_op jit(solution)/shard_map/air/pallas_call | solution.py:544
  44.1 72.2 %ocean.1 = (bf16[32,32,768]{2,1,0:T(8,128)(2,1)}, bf16[64,64,192]{2,1,0:T(8,128)(2,1)}) custom-call(bf16[16,4,8,256]{3,2,1,0:T(8,128)(2,1)} %get-tuple-element.4.table_ref, s32[4,64,64]{2,1,0:T(8,128)} %index_ref.1, f32[4,64,64]{2,1,0:T(8,128)} %remap_ref.1, f32[8,192]{1,0:T(8,128)} %lift_ref.1, bf16[64,64,192]{2,1,0:T(8,128)(2,1)} %ocean_ref.1, ...), custom_call_target="tpu_custom_call" | custom-call | flops 49999998976 | bytes 16777216 | tf_op jit(solution)/shard_map/ocean/pallas_call | solution.py:341
  116.3 0.0 copy-start
  116.3 2.8 %copy.23 = bf16[32,32,768]{2,1,0:T(8,128)(2,1)} copy(bf16[32,32,768]{2,1,0:T(8,128)(2,1)} %get-tuple-element.8) | data formatting | bytes 3145728
  119.1 0.0 copy-done
  119.1 1.3 %copy.24 = bf16[64,64,192]{2,1,0:T(8,128)(2,1)} copy(bf16[64,64,192]{2,1,0:T(8,128)(2,1)S(1)} %copy-done) | data formatting | bytes 3145728
Async XLA Ops:
  116.3 2.8 %copy-start = (bf16[64,64,192]{2,1,0:T(8,128)(2,1)S(1)}, bf16[64,64,192]{2,1,0:T(8,128)(2,1)}, u32[]{:S(2)}) copy-start(bf16[64,64,192]{2,1,0:T(8,128)(2,1)} %get-tuple-element.9) | copy-start | bytes 4718596

commit v4 on v3

--- a/solution.py
+++ b/solution.py
@@ -107,8 +107,9 @@
         total = jnp.zeros((8, CELLS), F32)
         for e in range(4):
             index = line(index_ref[e, pl.ds(pl.multiple_of(8 * i, 8), 8), :])
-            lo = (index & 24) << 3 | ((index >> 9) & 7) << 3 | (index & 7)
-            hi = jnp.broadcast_to((index >> 12) << 4 | ((index >> 5) & 15), (8, CELLS))
+            lo = ((index >> 12) & 1) << 7 | ((index >> 4) & 1) << 6 | ((index >> 9) & 7) << 3 | (index & 7)
+            edge = 1 - (((index >> 4) ^ (index >> 3)) & 1)
+            hi = jnp.broadcast_to(edge << 5 | (index >> 13) << 4 | ((index >> 5) & 15), (8, CELLS))
             hit = jnp.where(ids == lo, 1.0, 0.0).astype(BF)
             res = jnp.dot(t_ref[...], hit, preferred_element_type=F32)
             got = res[0:8]
@@ -296,7 +297,10 @@
                     warmth = pair(0) / jnp.maximum(pair(1), 1.0)
                     for j in range(CH):
                         r = 2 * j + s
-                        old = jnp.concatenate([second_ref[ci, 64 * c + 8 * r : 64 * c + 8 * r + 8, :] for c in range(4)], axis=0)
+                        start = [pl.multiple_of(128 * (ci % 2), 128) + 64 * (c // 2) + 8 * r for c in range(4)]
+                        old = jnp.concatenate(
+                            [second_ref[(2, 0, 0, 2)[c] + ci // 2, pl.ds(pl.multiple_of(start[c], 8), 8), :] for c in range(4)], axis=0
+                        )
                         row = jnp.concatenate([warmth[32 * j : 32 * j + 32]] * 6, axis=1)
                         updated_ref[8 * ci + r] = (old + row * embed_ref[...].reshape(1, 768)).astype(BF)
 
@@ -467,37 +471,41 @@
     def middle(band):
         for pair in range(6):
             q, k, v = pair_lanes(pair)
-            mixed[band, 64:192, q] = window(
+            mixed[0, band // 2, 128 * (band % 2) : 128 * (band % 2) + 128, q] = window(
                 [qkv[band, 1, :, k], qkv[band, 2, :, k]], [qkv[band, 1, :, v], qkv[band, 2, :, v]], [qkv[band, 1, :, q], qkv[band, 2, :, q]]
             )
 
     def edges(band):
+        base = 128 * (band % 2)
         for pair in range(6):
             q, k, v = pair_lanes(pair)
-            mixed[band, 0:64, q] = window(
+            mixed[1, band // 2, base : base + 64, q] = window(
                 [beside[0, band, :, q], qkv[band, 0, :, k]], [beside[0, band, :, k], qkv[band, 0, :, v]], [qkv[band, 0, :, q]]
             )
-            mixed[band, 192:256, q] = window(
+            mixed[1, band // 2, base + 64 : base + 128, q] = window(
                 [qkv[band, 3, :, k], beside[1, band, :, q]], [qkv[band, 3, :, v], beside[1, band, :, k]], [qkv[band, 3, :, q]]
             )
 
-    def feed_forward(band):
-        first = jnp.concatenate([cells(band, j) for j in range(4)], axis=0)
-        first = first + jnp.dot(mixed[band], out_w[...], preferred_element_type=F32)
+    def feed_forward(kind, pair):
+        first = stack(*[cells(2 * pair + band, j) for band in range(2) for j in ((1, 2), (0, 3))[kind]])
+        first = first + jnp.dot(mixed[kind, pair], out_w[...], preferred_element_type=F32)
         rows = rms(first, gain_mlp_ref[...].reshape(1, width))
         total = first
         for part in range(4):
             lanes = slice(width * part, width * part + width)
             hidden = gelu(jnp.dot(rows, up_w[:, lanes], preferred_element_type=F32)).astype(BF)
             total = total + jnp.dot(hidden, down_w[lanes, :], preferred_element_type=F32)
-        second_ref[band] = total
-        flux_ref[band] = lax.dot_general(head_ref[...], total.astype(BF), NT, preferred_element_type=F32).astype(BF)
-
-    def middle_step(band, _):
-        middle(band)
-        return 0
-
-    lax.fori_loop(0, 4, middle_step, 0)
+        second_ref[2 * kind + pair] = total
+        flux_ref[2 * kind + pair] = lax.dot_general(head_ref[...], total.astype(BF), NT, preferred_element_type=F32).astype(BF)
+
+    middle(0)
+    middle(1)
+    for load in loads[1:]:
+        load.wait()
+    feed_forward(0, 0)
+    middle(2)
+    middle(3)
+    feed_forward(0, 1)
     if comm:
         for copy in copies:
             copy.wait_recv()
@@ -512,18 +520,13 @@
 
     lax.fori_loop(0, 2, project_beside, 0)
     edges(0)
-    for load in loads[1:]:
-        load.wait()
-
-    def step(band, _):
-        feed_forward(band - 1)
-        edges(band)
-        return 0
-
-    lax.fori_loop(1, 4, step, 0)
+    edges(1)
+    feed_forward(1, 0)
     if comm:
         over_peers(0, lambda part, k: flux_copy(part, k).start())
-    feed_forward(3)
+    edges(2)
+    edges(3)
+    feed_forward(1, 1)
     if comm:
         over_peers(1, lambda part, k: flux_copy(part, k).start())
         table_ref[lon] = flux_ref[...]
@@ -552,7 +555,7 @@
             pltpu.VMEM((2, 4, 64, width), BF), pltpu.VMEM((2, 4, 64, width), BF),
             pltpu.VMEM((4, 4, 64, 3 * width), BF),
             pltpu.VMEM((2, 4, 64, 2 * width), BF),
-            pltpu.VMEM((4, 256, width), BF), pltpu.VMEM((4, 8, 256), BF),
+            pltpu.VMEM((2, 2, 256, width), BF), pltpu.VMEM((4, 8, 256), BF),
             pltpu.SemaphoreType.DMA((4,)), pltpu.SemaphoreType.DMA((2,)), pltpu.SemaphoreType.DMA((2,)),
             pltpu.SemaphoreType.DMA((2, 16)), pltpu.SemaphoreType.DMA((2, 16)),
         ],

time: 121 us -> 115 us (0.950)
  Pallas kernels: 116 us -> 110 us
    pallas_call x1, Pallas kernels: 43.5 us -> 37.1 us  [atmosphere(): pl.pallas_call(functools.partial(air_kernel, comm), out_shape=[jax.ShapeD...]
where the time goes in v4:
time: 115 us
  Pallas kernels  110 us (96%)
  local copies, waits for them, and re-layouts  4.12 us (4%)
    pallas_call x1, Pallas kernels, ocean_step(): pl.pallas_call(functools.partial(ocean_kernel, comm), out_shape=[jax.Shap...  72.9 us
    pallas_call x1, Pallas kernels, atmosphere(): pl.pallas_call(functools.partial(air_kernel, comm), out_shape=[jax.ShapeD...  37.1 us
    unnamed x4, local copies, waits for them, and re-layouts  4.12 us

profile of v4, /device:TPU:56, one launch (start us, length us, event | category | flops | bytes accessed | tf_op | source)
XLA Modules:
  0.0 114.8 jit_solution(8429953535135450235)
XLA Ops:
  0.6 37.1 %air.1 = (f32[4,256,768]{2,1,0:T(8,128)}, bf16[16,4,8,256]{3,2,1,0:T(8,128)(2,1)}) custom-call(bf16[4,8,32,768]{3,2,1,0:T(8,128)(2,1)} %bitcast.4, f32[768]{0:T(1024)} %gain_attn_ref.1, f32[768]{0:T(1024)} %gain_mlp_ref.1, bf16[768,2304]{1,0:T(8,128)(2,1)} %qkv_hbm.1, bf16[768,768]{1,0:T(8,128)(2,1)} %out_hbm.1, bf16[768,3072]{1,0:T(8,128)(2,1)} %up_hbm.1, ...), custom_call_target="tpu_custom_call" | custom-call | flops 16000000000 | bytes 20971520 | tf_op jit(solution)/shard_map/air/pallas_call | solution.py:547
  37.7 72.9 %ocean.1 = (bf16[32,32,768]{2,1,0:T(8,128)(2,1)}, bf16[64,64,192]{2,1,0:T(8,128)(2,1)}) custom-call(bf16[16,4,8,256]{3,2,1,0:T(8,128)(2,1)} %get-tuple-element.4.table_ref, s32[4,64,64]{2,1,0:T(8,128)} %index_ref.1, f32[4,64,64]{2,1,0:T(8,128)} %remap_ref.1, f32[8,192]{1,0:T(8,128)} %lift_ref.1, bf16[64,64,192]{2,1,0:T(8,128)(2,1)} %ocean_ref.1, ...), custom_call_target="tpu_custom_call" | custom-call | flops 49999998976 | bytes 16777216 | tf_op jit(solution)/shard_map/ocean/pallas_call | solution.py:345
  110.6 0.0 copy-start
  110.7 2.8 %copy.23 = bf16[32,32,768]{2,1,0:T(8,128)(2,1)} copy(bf16[32,32,768]{2,1,0:T(8,128)(2,1)} %get-tuple-element.8) | data formatting | bytes 3145728
  113.5 0.0 copy-done
  113.5 1.3 %copy.24 = bf16[64,64,192]{2,1,0:T(8,128)(2,1)} copy(bf16[64,64,192]{2,1,0:T(8,128)(2,1)S(1)} %copy-done) | data formatting | bytes 3145728
Async XLA Ops:
  110.6 2.8 %copy-start = (bf16[64,64,192]{2,1,0:T(8,128)(2,1)S(1)}, bf16[64,64,192]{2,1,0:T(8,128)(2,1)}, u32[]{:S(2)}) copy-start(bf16[64,64,192]{2,1,0:T(8,128)(2,1)} %get-tuple-element.9) | copy-start | bytes 4718596
